TPU v7x, 512 devices: a whole 4x4x16 slice. The times are simulated.
512 devices in a mesh: narrow: 16 (over y, x), wide: 32 (over z, core).
Axes of the slice: x: 4, y: 4, z: 16, core: 2. Of those that a mesh axis runs over, the one named last changes fastest.
Arguments:
- adjoint_rhs: float32 [32, 256, 760], P('wide', 'narrow'), may hold values from -1.8 to 1.8
- pivot_inverse: bfloat16 [32, 256, 9025], P('wide', 'narrow'), may hold values from -0.05 to 1.05
- upper_blocks: bfloat16 [32, 256, 9025], P('wide', 'narrow'), may hold values from -0.05 to 2.05
- lower_blocks: bfloat16 [32, 256, 9025], P('wide', 'narrow'), may hold values from -0.05 to 2.05
- face_neighbors: int32 [32, 2], P('wide'), may hold values from 0 to 31, as said below
- face_coupling: float32 [32, 256, 190], P('wide', 'narrow'), may hold values from 0.15 to 0.6
Outputs:
- first_apply: float32 [32, 256, 760], P('wide', 'narrow')
- second_apply: float32 [32, 256, 760], P('wide', 'narrow')
Inputs may be any that keep to these rules, and one draw needn't show every extreme that they name: `face_neighbors`: with the lines in blocks of 1 (block b holds lines b * 1 to (b + 1) - 1), both neighbors of a line of block b lie in blocks b - 1, b or b + 1, taken cyclically over the 32 lines.
All inputs are finite; a program needn't handle non-finite values.
Results may differ from a plain program's by a relative error of at most 0.0003.
Values sent between devices are 32-bit elements; how exact they have to be, the bound alone decides.
A program may use at most 64 MiB of HBM per device.

v0:
```python
import math

import jax
import jax.numpy as jnp
from jax import lax
from jax.sharding import PartitionSpec as P

NV = 95
NR = 8


exact_precision = lax.Precision.HIGHEST


def carried_in(value, axis, join, neutral, backward):
    count, mine = (lax.axis_size(axis), lax.axis_index(axis))
    pieces = jax.tree.map(lambda part: lax.all_gather(part, axis), value)
    if backward:
        pieces = jax.tree.map(lambda part: part[::-1], pieces)
        mine = count - 1 - mine
    so_far = jax.tree.map(
        lambda part, zero: jnp.full_like(part, 0) + jnp.asarray(zero, part.dtype), value, neutral
    )

    def turn(position, so_far):
        longer = join(so_far, jax.tree.map(lambda part: part[position], pieces))
        return jax.tree.map(lambda new, old: jnp.where(position < mine, new, old), longer, so_far)

    return lax.fori_loop(0, count - 1, turn, so_far)


def with_halo(block, sides, width):
    for axis, dim in sides:
        count = lax.axis_size(axis)
        forward = [(i, i + 1) for i in range(count - 1)]
        forward.append((count - 1, 0))
        backward = [(target, source) for source, target in forward]
        low = lax.ppermute(
            lax.slice_in_dim(block, block.shape[dim] - width, None, axis=dim), axis, forward
        )
        high = lax.ppermute(lax.slice_in_dim(block, 0, width, axis=dim), axis, backward)
        block = jnp.concatenate([low, block, high], axis=dim)
    return block


def adjoint_multiply(matrix_block, vector):
    return jnp.einsum(
        "...ba,...bk->...ak", matrix_block.astype(jnp.float32), vector, precision=exact_precision
    )


def plain_product(left_matrix, right_matrix):
    return jnp.einsum("...ab,...bk->...ak", left_matrix, right_matrix, precision=exact_precision)


def compose(earlier, later):
    return (plain_product(later[0], earlier[0]), plain_product(later[0], earlier[1]) + later[1])


def identity_map(line_count):
    unit_matrix = jnp.broadcast_to(jnp.eye(NV, dtype=jnp.float32), (line_count, NV, NV))
    return (unit_matrix, jnp.zeros((line_count, NV, NR), jnp.float32))


def in_cell_order(stacked, backward_sequence):
    flipped = stacked[::-1] if backward_sequence else stacked
    return jnp.moveaxis(flipped, 0, 2)


def widened_chain_solve(
    diagonal_submatrices, coupling_matrix_pieces, forcing_vector, backward_sequence
):
    line_count, segments, length = (
        forcing_vector.shape[0],
        forcing_vector.shape[1],
        forcing_vector.shape[2],
    )
    zero_carry = jnp.zeros((line_count, segments, NV, NR), jnp.float32)
    unit_matrix = jnp.broadcast_to(jnp.eye(NV, dtype=jnp.float32), (line_count, segments, NV, NV))
    carried_state = (zero_carry, unit_matrix)
    values_list = []
    response_list = []
    for step_index in range(length):
        location_within_chain = length - 1 - step_index if backward_sequence else step_index
        pivot_block = diagonal_submatrices[:, :, location_within_chain]
        coupling_matrix_piece = coupling_matrix_pieces[:, :, location_within_chain]
        source = forcing_vector[:, :, location_within_chain]
        numeric_elements = source - adjoint_multiply(pivot_block, carried_state[0])
        chain_solution = -adjoint_multiply(pivot_block, carried_state[1])
        carried_state = (
            adjoint_multiply(coupling_matrix_piece, numeric_elements),
            adjoint_multiply(coupling_matrix_piece, chain_solution),
        )
        values_list.append(numeric_elements)
        response_list.append(chain_solution)
    emitted_output = jnp.stack(values_list, axis=0)
    return (carried_state, emitted_output)


def plain_chain_solve(
    diagonal_submatrices,
    coupling_matrix_pieces,
    forcing_vector,
    chain_beginnings,
    backward_sequence,
):
    length = forcing_vector.shape[2]
    carried_state = chain_beginnings
    values_list = []
    for step_index in range(length):
        location_within_chain = length - 1 - step_index if backward_sequence else step_index
        pivot_block = diagonal_submatrices[:, :, location_within_chain]
        coupling_matrix_piece = coupling_matrix_pieces[:, :, location_within_chain]
        source = forcing_vector[:, :, location_within_chain]
        numeric_elements = source - adjoint_multiply(pivot_block, carried_state)
        carried_state = adjoint_multiply(coupling_matrix_piece, numeric_elements)
        values_list.append(numeric_elements)
    return (carried_state, jnp.stack(values_list, axis=0))


def chain_segments(matrices, offsets, backward_sequence):
    segments = matrices.shape[1]
    running = identity_map(matrices.shape[0])
    entries = [None] * segments
    visit_order = range(segments - 1, -1, -1) if backward_sequence else range(segments)
    for segment in visit_order:
        entries[segment] = running
        running = compose(running, (matrices[:, segment], offsets[:, segment]))
    stacked = (
        jnp.stack([entry[0] for entry in entries], axis=1),
        jnp.stack([entry[1] for entry in entries], axis=1),
    )
    return (stacked, running)


def device_prefix(combined, backward_sequence):
    identity = identity_map(combined[0].shape[0])
    if backward_sequence:
        return carried_in((combined[0], combined[1]), "narrow", compose, identity, True)
    return carried_in((combined[0], combined[1]), "narrow", compose, identity, False)


def directed_chain_solve(
    diagonal_submatrices, coupling_matrix_pieces, forcing_vector, backward_sequence
):
    carried_state, emitted_output = widened_chain_solve(
        diagonal_submatrices, coupling_matrix_pieces, forcing_vector, backward_sequence
    )
    entries, combined = chain_segments(carried_state[1], carried_state[0], backward_sequence)
    incoming = device_prefix(combined, backward_sequence)
    chain_beginnings = plain_product(entries[0], incoming[1][:, None]) + entries[1]
    unused_slot, repeated_output = plain_chain_solve(
        diagonal_submatrices,
        coupling_matrix_pieces,
        forcing_vector,
        chain_beginnings,
        backward_sequence,
    )
    return (in_cell_order(repeated_output, backward_sequence), None)


def apply_preconditioner(source_cells, diagonal_submatrices, uppers, lowers):
    fore_kept = None
    back_kept = None
    scaled_source = adjoint_multiply(diagonal_submatrices, source_cells)
    forward, fore_kept = directed_chain_solve(diagonal_submatrices, uppers, scaled_source, False)
    result, back_kept = directed_chain_solve(diagonal_submatrices, lowers, forward, True)
    return (result, (fore_kept, back_kept))


def body(adjoint_rhs, pivot_inverse, upper_blocks, lower_blocks, face_neighbors, face_coupling):
    line_count, cell_count = (adjoint_rhs.shape[0], adjoint_rhs.shape[1])
    length = math.gcd(cell_count, 8)
    segments = cell_count // length
    diagonal_submatrices = pivot_inverse.reshape(line_count, segments, length, NV, NV)
    uppers = upper_blocks.reshape(line_count, segments, length, NV, NV)
    lowers = lower_blocks.reshape(line_count, segments, length, NV, NV)
    source_cells = adjoint_rhs.reshape(line_count, segments, length, NV, NR)
    first_cells, kept = apply_preconditioner(source_cells, diagonal_submatrices, uppers, lowers)
    first_result = first_cells.reshape(line_count, cell_count, NV * NR)
    window = with_halo(first_result, (("wide", 0),), line_count)
    start_line = lax.axis_index("wide") * line_count
    total_lines = line_count * lax.axis_size("wide")
    relative = (face_neighbors - start_line + line_count) % total_lines
    candidates = jnp.arange(3 * line_count, dtype=jnp.int32)
    selector = (relative[:, :, None] == candidates[None, None, :]).astype(jnp.float32)
    picked = jnp.einsum("lsm,mcv->lscv", selector, window, precision=exact_precision).reshape(
        line_count, 2, cell_count, NV, NR
    )
    coefficients = face_coupling.reshape(line_count, cell_count, 2, NV)
    coupled = (
        coefficients[:, :, 0, :, None] * picked[:, 0]
        + coefficients[:, :, 1, :, None] * picked[:, 1]
    )
    second_source = adjoint_rhs.reshape(line_count, cell_count, NV, NR) - coupled
    second, unused_slot = apply_preconditioner(
        second_source.reshape(line_count, segments, length, NV, NR),
        diagonal_submatrices,
        uppers,
        lowers,
    )
    return (first_result, second.reshape(line_count, cell_count, NV * NR))


def solution(mesh):
    return jax.shard_map(
        body,
        mesh=mesh,
        in_specs=(
            P("wide", "narrow", None),
            P("wide", "narrow", None),
            P("wide", "narrow", None),
            P("wide", "narrow", None),
            P("wide", None),
            P("wide", "narrow", None),
        ),
        out_specs=(P("wide", "narrow", None), P("wide", "narrow", None)),
        check_vma=False,
    )
```

profile of v0, /device:TPU:24, one launch (start us, length us, event | category | flops | bytes accessed | tf_op | source)
XLA Modules:
  0.0 258.6 jit_solution(4068409486191420117)
XLA Ops:
  0.7 2.3 reshape.1324
  3.7 1.3 reshape.1326
  8.2 1.3 reshape.1347
  13.3 1.3 reshape.1322
  18.7 27.0 %all-gather.6 = f32[16,95,95]{2,1,0:T(8,128)S(1)} all-gather(f32[1,95,95]{2,1,0:T(8,128)S(1)} %convolution_bitcast_fusion.6), channel_id=2, replica_groups=mesh['narrow'=16,'wide'=32] {'narrow'}, dimensions={0}, use_global_device_ids=true | all-gather | bytes 613700 | tf_op jit(solution)/shard_map/all_gather | solution.py:17
  45.7 20.7 %all-gather.7 = f32[16,95,8]{1,2,0:T(8,128)S(1)} all-gather(f32[1,95,8]{1,2,0:T(8,128)S(1)} %fusion.119), channel_id=3, replica_groups=mesh['narrow'=16,'wide'=32] {'narrow'}, dimensions={0}, use_global_device_ids=true | all-gather | bytes 51680 | tf_op jit(solution)/shard_map/all_gather | solution.py:17
  66.4 3.1 %while.56 = (s32[]{:T(128)}, f32[1,95,8]{1,2,0:T(8,128)S(1)}, s32[]{:T(128)}, f32[16,1,95,95]{3,2,1,0:T(8,128)S(1)}, f32[16,1,95,8]{2,3,1,0:T(8,128)S(1)}, /*index=5*/s32[]{:T(128)}, s32[]{:T(128)}) while((s32[]{:T(128)}, f32[1,95,8]{1,2,0:T(8,128)S(1)}, s32[]{:T(128)}, f32[16,1,95,95]{3,2,1,0:T(8,128)S(1)}, ...), condition=%wide.region_1.2_spmd.clone, body=%wide.region_0.1_spmd.clone.sunk | while | flops 869444 | bytes 73223 | solution.py:29
  87.0 24.4 %all-gather.8 = f32[16,95,95]{2,1,0:T(8,128)S(1)} all-gather(f32[1,95,95]{2,1,0:T(8,128)S(1)} %convolution_bitcast_fusion.5), channel_id=4, replica_groups=mesh['narrow'=16,'wide'=32] {'narrow'}, dimensions={0}, use_global_device_ids=true | all-gather | bytes 613700 | tf_op jit(solution)/shard_map/all_gather | solution.py:17
  111.5 20.9 %all-gather.9 = f32[16,95,8]{1,2,0:T(8,128)S(1)} all-gather(f32[1,95,8]{1,2,0:T(8,128)S(1)} %fusion.118), channel_id=5, replica_groups=mesh['narrow'=16,'wide'=32] {'narrow'}, dimensions={0}, use_global_device_ids=true | all-gather | bytes 51680 | tf_op jit(solution)/shard_map/all_gather | solution.py:17
  132.3 3.1 %while.57 = (s32[]{:T(128)}, f32[1,95,8]{1,2,0:T(8,128)S(1)}, s32[]{:T(128)}, f32[16,1,95,95]{3,2,1,0:T(8,128)S(1)}, f32[16,1,95,8]{2,3,1,0:T(8,128)S(1)}, /*index=5*/s32[]{:T(128)}, s32[]{:T(128)}) while((s32[]{:T(128)}, f32[1,95,8]{1,2,0:T(8,128)S(1)}, s32[]{:T(128)}, f32[16,1,95,95]{3,2,1,0:T(8,128)S(1)}, ...), condition=%wide.region_3.4_spmd.clone, body=%wide.region_2.3_spmd.clone.sunk | while | flops 869444 | bytes 73223 | solution.py:29
  140.7 7.5 %collective-permute-done = f32[1,16,760]{2,1,0:T(8,128)S(1)} collective-permute-done((f32[1,16,760]{2,1,0:T(8,128)S(1)}, f32[1,16,760]{2,1,0:T(8,128)S(1)}, u32[]{:S(2)}, u32[]{:S(2)}) %collective-permute-start) | collective-permute-done | bytes 48672 | tf_op jit(solution)/shard_map/ppermute | solution.py:38
  152.7 22.9 %all-gather.10 = f32[16,95,8]{1,2,0:T(8,128)S(1)} all-gather(f32[1,95,8]{1,2,0:T(8,128)S(1)} %fusion.117), channel_id=6, replica_groups=mesh['narrow'=16,'wide'=32] {'narrow'}, dimensions={0}, use_global_device_ids=true | all-gather | bytes 51680 | tf_op jit(solution)/shard_map/all_gather | solution.py:17
  175.6 15.0 %while.58 = (s32[]{:T(128)}, f32[1,95,8]{1,2,0:T(8,128)S(1)}, s32[]{:T(128)}, f32[16,1,95,95]{3,2,1,0:T(8,128)}, f32[16,1,95,8]{2,3,1,0:T(8,128)S(1)}, /*index=5*/s32[]{:T(128)}, s32[]{:T(128)}) while((s32[]{:T(128)}, f32[1,95,8]{1,2,0:T(8,128)S(1)}, s32[]{:T(128)}, f32[16,1,95,95]{3,2,1,0:T(8,128)}, ...), condition=%wide.region_5.6_spmd.clone, body=%wide.region_4.5_spmd.clone.sunk | while | flops 869444 | bytes 73223 | solution.py:29
  179.6 1.0 fusion.411
  180.6 1.0 fusion.411
  181.6 1.0 fusion.411
  186.6 1.0 fusion.411
  187.6 1.0 fusion.411
  206.9 21.5 %all-gather.11 = f32[16,95,8]{1,2,0:T(8,128)S(1)} all-gather(f32[1,95,8]{1,2,0:T(8,128)S(1)} %fusion.116), channel_id=7, replica_groups=mesh['narrow'=16,'wide'=32] {'narrow'}, dimensions={0}, use_global_device_ids=true | all-gather | bytes 51680 | tf_op jit(solution)/shard_map/all_gather | solution.py:17
  228.4 15.1 %while.59 = (s32[]{:T(128)}, f32[1,95,8]{1,2,0:T(8,128)S(1)}, s32[]{:T(128)}, f32[16,1,95,95]{3,2,1,0:T(8,128)}, f32[16,1,95,8]{2,3,1,0:T(8,128)S(1)}, /*index=5*/s32[]{:T(128)}, s32[]{:T(128)}) while((s32[]{:T(128)}, f32[1,95,8]{1,2,0:T(8,128)S(1)}, s32[]{:T(128)}, f32[16,1,95,95]{3,2,1,0:T(8,128)}, ...), condition=%wide.region_7.8_spmd.clone, body=%wide.region_6.7_spmd.clone.sunk | while | flops 869444 | bytes 73223 | solution.py:29
  230.5 1.0 fusion.414
  231.5 1.0 fusion.414
  236.5 1.0 fusion.414
  257.6 1.0 reshape.1367
  (375 shorter events, 97.2 us)
Async XLA Ops:
  0.7 134.8 %copy-start.7 = (f32[1,1,95,95]{3,2,1,0:T(8,128)}, f32[1,1,95,95]{3,2,1,0:T(8,128)S(1)}, u32[]{:S(2)}) copy-start(f32[1,1,95,95]{3,2,1,0:T(8,128)S(1)} %fusion.127) | copy-start | bytes 108304
  3.0 66.8 %copy-start = (bf16[1,2,8,95,95]{4,3,2,1,0:T(8,128)(2,1)}, bf16[1,2,8,95,95]{4,3,2,1,0:T(8,128)(2,1)S(1)}, u32[]{:S(2)}) copy-start(bf16[1,2,8,95,95]{4,3,2,1,0:T(8,128)(2,1)S(1)} %reshape.1324) | copy-start | bytes 866404
  5.0 13.1 %copy-start.3 = (bf16[1,2,8,95,95]{4,3,2,1,0:T(8,128)(2,1)}, bf16[1,2,8,95,95]{4,3,2,1,0:T(8,128)(2,1)S(1)}, u32[]{:S(2)}) copy-start(bf16[1,2,8,95,95]{4,3,2,1,0:T(8,128)(2,1)S(1)} %reshape.1326) | copy-start | bytes 866404
  7.8 10.6 %copy-start.13 = (f32[1,2,95,95]{2,3,1,0:T(8,128)}, f32[1,2,95,95]{2,3,1,0:T(8,128)S(1)}, u32[]{:S(2)}) copy-start(f32[1,2,95,95]{2,3,1,0:T(8,128)S(1)} %convolution_bitcast_fusion.2) | copy-start | bytes 216604
  7.9 10.4 %copy-start.26 = (f32[95,8]{0,1:T(8,128)}, f32[95,8]{0,1:T(8,128)S(1)}, u32[]{:S(2)}) copy-start(f32[95,8]{0,1:T(8,128)S(1)} %fusion.128) | copy-start | bytes 9124
  8.2 10.2 %copy-start.17 = (f32[95,95]{1,0:T(8,128)}, f32[95,95]{1,0:T(8,128)S(1)}, u32[]{:S(2)}) copy-start(f32[95,95]{1,0:T(8,128)S(1)} %fusion.125) | copy-start | bytes 108304
  9.5 197.1 %copy-start.2 = (bf16[1,2,8,95,95]{4,3,2,1,0:T(8,128)(2,1)}, bf16[1,2,8,95,95]{4,3,2,1,0:T(8,128)(2,1)S(1)}, u32[]{:S(2)}) copy-start(bf16[1,2,8,95,95]{4,3,2,1,0:T(8,128)(2,1)S(1)} %reshape.1347) | copy-start | bytes 866404
  11.2 3.4 %copy-start.28 = (f32[1,16,760]{2,1,0:T(8,128)S(1)}, f32[1,16,760]{2,1,0:T(8,128)}, u32[]{:S(2)}) copy-start(f32[1,16,760]{2,1,0:T(8,128)} %param.14) | copy-start | bytes 145924
  15.8 54.0 %copy-start.20 = (f32[1,2,8,95,8]{3,4,2,1,0:T(8,128)}, f32[1,2,8,95,8]{3,4,2,1,0:T(8,128)S(1)}, u32[]{:S(2)}) copy-start(f32[1,2,8,95,8]{3,4,2,1,0:T(8,128)S(1)} %convolution_bitcast_fusion.3) | copy-start | bytes 145924
  18.6 50.8 %copy-start.18 = (f32[95,95]{1,0:T(8,128)S(1)}, f32[95,95]{1,0:T(8,128)}, u32[]{:S(2)}) copy-start(f32[95,95]{1,0:T(8,128)} %copy-done.17) | copy-start | bytes 108304
  69.4 17.2 %copy-start.6 = (f32[16,1,95,95]{3,2,1,0:T(8,128)}, f32[16,1,95,95]{3,2,1,0:T(8,128)S(1)}, u32[]{:S(2)}) copy-start(f32[16,1,95,95]{3,2,1,0:T(8,128)S(1)} %get-tuple-element.843) | copy-start | bytes 1732804
  69.4 17.1 %copy-start.11 = (f32[1,2,95,95]{2,3,1,0:T(8,128)S(1)}, f32[1,2,95,95]{2,3,1,0:T(8,128)}, u32[]{:S(2)}) copy-start(f32[1,2,95,95]{2,3,1,0:T(8,128)} %copy-done.10) | copy-start | bytes 216604
  69.5 17.2 %copy-start.15 = (f32[95,95]{1,0:T(8,128)S(1)}, f32[95,95]{1,0:T(8,128)}, u32[]{:S(2)}) copy-start(f32[95,95]{1,0:T(8,128)} %fusion.124) | copy-start | bytes 108304
  70.0 14.7 %copy-start.1 = (bf16[1,2,8,95,95]{4,3,2,1,0:T(8,128)(2,1)S(1)}, bf16[1,2,8,95,95]{4,3,2,1,0:T(8,128)(2,1)}, u32[]{:S(2)}) copy-start(bf16[1,2,8,95,95]{4,3,2,1,0:T(8,128)(2,1)} %copy-done) | copy-start | bytes 866404
  138.9 9.7 %copy-start.25 = (f32[1,16,760]{2,1,0:T(8,128)}, f32[1,16,760]{2,1,0:T(8,128)S(1)}, u32[]{:S(2)}) copy-start(f32[1,16,760]{2,1,0:T(8,128)S(1)} %reshape.1361) | copy-start | bytes 145924
  138.9 1.8 collective-permute-start.1
  138.9 9.2 %collective-permute-start = (f32[1,16,760]{2,1,0:T(8,128)S(1)}, f32[1,16,760]{2,1,0:T(8,128)S(1)}, u32[]{:S(2)}, u32[]{:S(2)}) collective-permute-start(f32[1,16,760]{2,1,0:T(8,128)S(1)} %reshape.1361), channel_id=1, source_target_pairs={{0,1},{1,2},{2,3},{3,4},{4,5},{5,6},{6,7},{7,8},{8,9},{9,10},{10,1... | collective-permute-start | bytes 145928 | tf_op jit(solution)/shard_map/ppermute | solution.py:38
  149.2 3.3 %copy-start.14 = (f32[1,2,95,95]{2,3,1,0:T(8,128)S(1)}, f32[1,2,95,95]{2,3,1,0:T(8,128)}, u32[]{:S(2)}) copy-start(f32[1,2,95,95]{2,3,1,0:T(8,128)} %copy-done.13) | copy-start | bytes 216604
  149.8 40.9 %copy-start.8 = (f32[1,1,95,95]{3,2,1,0:T(8,128)S(1)}, f32[1,1,95,95]{3,2,1,0:T(8,128)}, u32[]{:S(2)}) copy-start(f32[1,1,95,95]{3,2,1,0:T(8,128)} %copy-done.7) | copy-start | bytes 108304
  149.8 40.9 %copy-start.19 = (f32[95,95]{1,0:T(8,128)S(1)}, f32[95,95]{1,0:T(8,128)}, u32[]{:S(2)}) copy-start(f32[95,95]{1,0:T(8,128)} %copy-done.17) | copy-start | bytes 108304
  150.2 41.9 %copy-start.21 = (f32[1,2,8,95,8]{3,4,1,2,0:T(8,128)}, f32[1,2,8,95,8]{3,4,1,2,0:T(8,128)S(1)}, u32[]{:S(2)}) copy-start(f32[1,2,8,95,8]{3,4,1,2,0:T(8,128)S(1)} %convolution_bitcast_fusion.4) | copy-start | bytes 145924
  190.7 16.1 %copy-start.12 = (f32[1,2,95,95]{2,3,1,0:T(8,128)S(1)}, f32[1,2,95,95]{2,3,1,0:T(8,128)}, u32[]{:S(2)}) copy-start(f32[1,2,95,95]{2,3,1,0:T(8,128)} %copy-done.10) | copy-start | bytes 216604
  198.8 44.7 %copy-start.16 = (f32[95,95]{1,0:T(8,128)S(1)}, f32[95,95]{1,0:T(8,128)}, u32[]{:S(2)}) copy-start(f32[95,95]{1,0:T(8,128)} %fusion.124) | copy-start | bytes 108304
  204.4 40.5 %copy-start.22 = (f32[8,1,2,95,8]{3,4,2,0,1:T(8,128)}, f32[8,1,2,95,8]{3,4,2,0,1:T(8,128)S(1)}, u32[]{:S(2)}) copy-start(f32[8,1,2,95,8]{3,4,2,0,1:T(8,128)S(1)} %fusion.61) | copy-start | bytes 145924
  (9 other events, 21.3 us)
where the time goes:
time: 263 us; the launch traced here: 259 us
  blocking collectives  137 us (52%)
  matrix products  100 us (38%)
  local copies, waits for them, and re-layouts  10.7 us (4%)
  waiting for transfers between devices  8.33 us (3%)
    all_gather x6, blocking collectives, carried_in(): pieces = jax.tree.map(lambda part: lax.all_gather(part, axis), value)  137 us
    dot_general x156, matrix products, adjoint_multiply(): jnp.einsum('...ba,...bk->...ak', matrix_block.astype(jnp.float32), vector...  60.4 us
    dot_general x74, matrix products, plain_product(): jnp.einsum('...ab,...bk->...ak', left_matrix, right_matrix, precision=exa...  39.4 us
    ppermute x1, waiting for transfers between devices, with_halo(): lax.ppermute(lax.slice_in_dim(block, block.shape[dim] - width, None, axis...  7.49 us
  transfers between devices with their start and end apart: 2, of which 2 were waited for; matrix products, arithmetic and copies ran while one was open for 0% of the time, Pallas kernels for 0%

commit v1 on v0

v1 whole, which is shorter than its diff:
```python
import functools

import jax
import jax.numpy as jnp
from jax import lax
from jax.experimental import pallas as pl
from jax.experimental.pallas import tpu as pltpu
from jax.sharding import PartitionSpec as P

NV = 95
NR = 8
ROWS = 96
PACKED = 72
LANES = 128
F32 = jnp.float32
BF16 = jnp.bfloat16
MESH = pl.DeviceIdType.MESH


def dot(left, right):
    return jnp.dot(left, right, preferred_element_type=F32)


def parts(value):
    high = value.astype(BF16)
    return high, (value - high.astype(F32)).astype(BF16)


def stacked_vector(value):
    high = value.astype(BF16).astype(F32)
    return jnp.concatenate([high, value - high], axis=0).astype(BF16)


def folded(product):
    rows = product.shape[0] // 2
    return product[:rows, :LANES] + (product[:rows, LANES:] + product[rows:, :LANES])


def put(ref, index, value):
    high, low = parts(value)
    ref[index, pl.ds(0, ROWS), pl.ds(0, LANES)] = high
    ref[index, pl.ds(0, ROWS), pl.ds(LANES, LANES)] = low


def left_of(place):
    ref, index = place
    return ref[index, pl.ds(0, ROWS), :]


def right_of(place):
    ref, index = place
    value = ref[index]
    return jnp.concatenate([value, value], axis=0)


def multiply(left, right):
    product = dot(left, right)
    return product[:, :LANES] + product[:, LANES:]


def packed(value):
    top, rest = value[:PACKED], value[PACKED:]
    lane = lax.broadcasted_iota(jnp.int32, rest.shape, 1)
    pieces = []
    for part in range(3):
        moved = pltpu.roll(rest, (ROWS - 32 * part) % LANES, 1)
        pieces.append(jnp.where(lane >= ROWS, moved, top[24 * part : 24 * part + 24]))
    return jnp.concatenate(pieces, axis=0)


def unpacked(value):
    lane = lax.broadcasted_iota(jnp.int32, (24, LANES), 1)
    rest = jnp.zeros((24, LANES), F32)
    pieces = []
    for part in range(3):
        own = value[24 * part : 24 * part + 24]
        moved = pltpu.roll(own, (LANES - ROWS + 32 * part) % LANES, 1)
        rest = jnp.where((lane >= 32 * part) & (lane < 32 * part + 32), moved, rest)
        pieces.append(jnp.where(lane < ROWS, own, 0.0))
    return jnp.concatenate(pieces + [rest], axis=0)


def granule_transpose(value):
    row = lax.broadcasted_iota(jnp.int32, value.shape, 0)
    group = lax.broadcasted_iota(jnp.int32, value.shape, 1) // NR
    height = value.shape[0]
    for bit in (1, 2, 4, 8):
        row_set = (row & bit) != 0
        group_set = (group & bit) != 0
        down = pltpu.roll(pltpu.roll(value, bit, 0), LANES - NR * bit, 1)
        up = pltpu.roll(pltpu.roll(value, height - bit, 0), NR * bit, 1)
        value = jnp.where(row_set == group_set, value, jnp.where(row_set, down, up))
    return value


def load_cells(flat_ref, pad_ref):
    cells = flat_ref.shape[0]
    width = NV * NR
    pad_ref[...] = jnp.zeros_like(pad_ref)
    for block in range(ROWS // 16):
        first = block * LANES
        wide = min(LANES, width - first)
        pad_ref[pl.ds(block * 16, cells), pl.ds(0, wide)] = flat_ref[:, pl.ds(first, wide)]
    turned = granule_transpose(pad_ref[pl.ds(0, ROWS), :])
    pad_ref[pl.ds(0, ROWS), :] = turned
    return jnp.transpose(pad_ref[...])


def store_cells(blocks, flat_ref):
    width = NV * NR
    cells = flat_ref.shape[0]
    turned = granule_transpose(jnp.transpose(blocks)[:ROWS])
    for block in range(ROWS // 16):
        first = block * LANES
        wide = min(LANES, width - first)
        flat_ref[:, pl.ds(first, wide)] = turned[block * 16 : block * 16 + cells, :wide]


def low_bit(m):
    return m & -m


def node(level_size, cells, first):
    return 2 * cells - 2 * cells // level_size + first // level_size


def kernel(
    n,
    lines,
    pivot_hbm,
    upper_hbm,
    lower_hbm,
    rhs_hbm,
    face_ref,
    coef_hbm,
    first_ref,
    second_ref,
    flat,
    rhs_ref,
    coef_ref,
    slab,
    pad,
    pivot,
    tn,
    tb,
    qw,
    ew,
    kw,
    jw,
    jp,
    hw,
    maps,
    came,
    phi,
    src,
    zs,
    us,
    xs,
    halo,
    fsend,
    gsend,
    fcame,
    gcame,
    load_sem,
    map_out,
    map_in,
    f_out,
    f_in,
    g_out,
    g_in,
    halo_out,
    halo_in,
):
    cells = rhs_ref.shape[0]
    me = lax.axis_index("narrow")
    line = lax.axis_index("wide")
    low_line = lax.rem(line + lines - 1, lines)
    high_line = lax.rem(line + 1, lines)

    loads = [
        pltpu.make_async_copy(hbm, flat.at[number], load_sem.at[number])
        for number, hbm in enumerate((pivot_hbm, upper_hbm, lower_hbm))
    ]
    loads.append(pltpu.make_async_copy(rhs_hbm, rhs_ref, load_sem.at[3]))
    loads.append(pltpu.make_async_copy(coef_hbm, coef_ref, load_sem.at[4]))
    for load in loads:
        load.start()

    fcame[...] = jnp.zeros_like(fcame)
    gcame[...] = jnp.zeros_like(gcame)

    barrier = pltpu.get_barrier_semaphore()

    def greet(step, _):
        pl.semaphore_signal(
            barrier, inc=1, device_id={"narrow": lax.rem(me + step, n)}, device_id_type=MESH
        )
        return 0

    lax.fori_loop(1, n, greet, 0)
    for other in (low_line, high_line):
        pl.semaphore_signal(barrier, inc=1, device_id={"wide": other}, device_id_type=MESH)

    slab[...] = jnp.zeros_like(slab)
    tail = jnp.zeros((LANES - ROWS, 2 * LANES), BF16)

    def clear_nodes(i, _):
        for ref in (tn, tb):
            ref[i, pl.ds(ROWS, LANES - ROWS), :] = tail
        return 0

    lax.fori_loop(0, 2 * cells - 1, clear_nodes, 0)

    def clear(i, _):
        for ref in (qw, ew, kw, jw, jp):
            ref[i, pl.ds(ROWS, LANES - ROWS), :] = tail
        return 0

    lax.fori_loop(0, cells, clear, 0)
    hw[0, pl.ds(ROWS, LANES - ROWS), :] = tail

    def clear_phi(i, _):
        phi[i] = jnp.zeros((LANES, 2 * LANES), BF16)
        return 0

    lax.fori_loop(0, n, clear_phi, 0)

    for number in range(3):
        loads[number].wait()
        for row in range(NV):
            slab[number, pl.ds(row * cells, cells), pl.ds(0, NV)] = flat[
                number, :, pl.ds(row * NV, NV)
            ].astype(F32)

    no_rows = jnp.zeros((LANES - ROWS, LANES), BF16)
    together = 4

    def multiply_blocks(group, _):
        for member in range(together):
            i = group * together + member
            p, u, l = (
                slab[number, pl.ds(i, ROWS, stride=cells), :] for number in range(3)
            )
            p16 = p.astype(BF16)
            pivot[i] = jnp.concatenate([p16, no_rows], axis=0)
            right = jnp.concatenate([(-u).astype(BF16), (-l).astype(BF16)], axis=1)
            right = jnp.concatenate([right, tail], axis=0)
            both = dot(p16, right)
            put(tn, i, both[:, :LANES])
            put(tb, i, both[:, LANES:])
        return 0

    lax.fori_loop(0, cells // together, multiply_blocks, 0)

    def join(place):
        forward = multiply(left_of((tn, 2 * place)), right_of((tn, 2 * place + 1)))
        backward = multiply(left_of((tb, 2 * place + 1)), right_of((tb, 2 * place)))
        return forward, backward

    def join_group(group, _):
        for member in range(together):
            place = group * together + member
            forward, backward = join(place)
            put(tn, cells + place, forward)
            put(tb, cells + place, backward)
        return 0

    last = cells - 2
    grouped = (cells - 4) // together
    lax.fori_loop(0, grouped, join_group, 0)
    for place in range(grouped * together, last):
        forward, backward = join(place)
        put(tn, cells + place, forward)
        put(tb, cells + place, backward)
    forward, backward = join(last)
    maps[0] = packed(forward)
    maps[1] = packed(backward)

    pl.semaphore_wait(barrier, n - 1 + 2)

    def map_copy(which, slot, target):
        return pltpu.make_async_remote_copy(
            src_ref=maps.at[which],
            dst_ref=came.at[slot],
            send_sem=map_out.at[slot],
            recv_sem=map_in.at[slot],
            device_id={"narrow": target},
            device_id_type=MESH,
        )

    def send_maps(step, _):
        @pl.when((me >= 1) & (me + step < n))
        def _():
            map_copy(0, step, me + step).start()

        @pl.when((me <= n - 2) & (me - step >= 0))
        def _():
            map_copy(1, n - step, me - step).start()

        return 0

    lax.fori_loop(1, n, send_maps, 0)
    put(tn, cells + last, forward)
    put(tb, cells + last, backward)

    def offset_copy(source, target_ref, turn, slot, out, arrived, target):
        return pltpu.make_async_remote_copy(
            src_ref=source.at[turn],
            dst_ref=target_ref.at[turn, slot],
            send_sem=out.at[turn, slot],
            recv_sem=arrived.at[turn, slot],
            device_id={"narrow": target},
            device_id_type=MESH,
        )

    def f_copy(turn, slot, target):
        return offset_copy(fsend, fcame, turn, slot, f_out, f_in, target)

    def g_copy(turn, slot, target):
        return offset_copy(gsend, gcame, turn, slot, g_out, g_in, target)

    def send_f(turn):
        def send(step, _):
            @pl.when(me + step < n)
            def _():
                f_copy(turn, step, me + step).start()

            return 0

        lax.fori_loop(1, n, send, 0)

    def send_g(turn):
        def send(step, _):
            @pl.when(me - step >= 0)
            def _():
                g_copy(turn, n - step, me - step).start()

            return 0

        lax.fori_loop(1, n, send, 0)

    def wait_f(turn):
        def wait(step, _):
            @pl.when(step <= me)
            def _():
                f_copy(turn, step, me).wait_recv()

            return 0

        lax.fori_loop(1, n, wait, 0)

    def wait_g(turn):
        def wait(step, _):
            @pl.when(me + step < n)
            def _():
                g_copy(turn, n - step, me).wait_recv()

            return 0

        lax.fori_loop(1, n, wait, 0)

    def deep(vectors, weights):
        left = jnp.concatenate([stacked_vector(v) for v in vectors], axis=1)
        right = jnp.concatenate([ref[index] for ref, index in weights], axis=0)
        return folded(dot(left, right))

    def by(vector, place):
        ref, index = place
        return folded(dot(stacked_vector(vector), ref[index]))

    def first_n(m):
        return (tn, node(m, cells, 0)) if m and low_bit(m) == m else (kw, m)

    def last_n(m):
        return (tn, node(m, cells, cells - m)) if low_bit(m) == m else (qw, m)

    def last_b(m):
        return (tb, node(m, cells, cells - m)) if m and low_bit(m) == m else (jw, m)

    def first_b(m):
        return (tb, node(m, cells, 0)) if low_bit(m) == m else (ew, m)

    row = lax.broadcasted_iota(jnp.int32, (ROWS, LANES), 0)
    column = lax.broadcasted_iota(jnp.int32, (ROWS, LANES), 1)
    unit = jnp.where((row == column) & (row < NV), 1.0, 0.0).astype(F32)
    put(kw, 0, unit)
    put(jw, 0, unit)

    loads[3].wait()
    blocks = load_cells(rhs_ref, pad)
    for i in range(cells):
        src[i] = blocks[i * NR : (i + 1) * NR]

    mixed = [m for m in range(1, cells) if low_bit(m) != m]
    for m in mixed:
        size = low_bit(m)
        at_end = node(size, cells, m - size)
        at_start = node(size, cells, cells - m)
        put(qw, m, multiply(left_of((tn, at_start)), right_of(last_n(m - size))))
        put(ew, m, multiply(left_of((tb, at_end)), right_of(first_b(m - size))))

    suffixes = [last_n(cells - i) for i in range(cells)]
    prefixes = [first_b(i + 1) for i in range(cells)]

    fsend[0] = deep([src[i] for i in range(cells)], suffixes)
    send_f(0)

    for m in mixed:
        size = low_bit(m)
        at_end = node(size, cells, m - size)
        at_start = node(size, cells, cells - m)
        put(kw, m, multiply(left_of(first_n(m - size)), right_of((tn, at_end))))
        put(jw, m, multiply(left_of(last_b(m - size)), right_of((tb, at_start))))

    response = multiply(
        jnp.concatenate([left_of(first_n(i)) for i in range(cells)], axis=1),
        jnp.concatenate([right_of(first_b(i + 1)) for i in range(cells)], axis=0),
    )
    put(hw, 0, response)
    for i in range(cells):
        exact = pivot[i]
        put(jp, i, dot(left_of(last_b(cells - 1 - i)), jnp.concatenate([exact, exact], axis=0)))

    def sweep():
        def forward(i, z):
            z = src[i] + by(z, (tn, i - 1))
            zs[i] = z
            return z

        zs[0] = src[0]
        lax.fori_loop(1, cells, forward, src[0])

    sweep()

    @pl.when(me >= 1)
    def _():
        put(phi, 1, unit)

    @pl.when(me <= n - 2)
    def _():
        put(phi, n - 1, unit)

    def extend(slot, towards):
        high, low = parts(unpacked(came[slot]))
        put(phi, towards, multiply(jnp.concatenate([high, low], axis=1), right_of((phi, slot))))

    def chain(step, _):
        @pl.when(step <= me - 1)
        def _():
            map_copy(0, step, me).wait_recv()
            extend(step, step + 1)

        @pl.when(step <= n - 2 - me)
        def _():
            map_copy(1, n - step, me).wait_recv()
            extend(n - step, n - step - 1)

        return 0

    lax.fori_loop(1, n - 1, chain, 0)

    between = [(phi, k) for k in range(n)]

    def finish(turn):
        alone = deep([zs[i] for i in range(cells)], prefixes)
        wait_f(turn)
        entering = deep([fcame[turn, k] for k in range(n)], between)
        left = stacked_vector(entering)
        gsend[turn] = alone + folded(dot(left, hw[0]))
        send_g(turn)
        for i in range(cells):
            ref, index = first_n(i)
            zs[i] = zs[i] + folded(dot(left, ref[index]))
        us[cells - 1] = zs[cells - 1]

        def backward(i, u):
            back = cells - 1 - i
            u = zs[back] + by(u, (tb, back + 1))
            us[back] = u
            return u

        lax.fori_loop(1, cells, backward, zs[cells - 1])
        for i in range(cells):
            product = dot(stacked_vector(us[i]), pivot[i])
            xs[turn, i] = product[:NR] + product[NR:]
        wait_g(turn)
        entering = deep([gcame[turn, k] for k in range(n)], between)
        left = stacked_vector(entering)
        for i in range(cells):
            xs[turn, i] = xs[turn, i] + folded(dot(left, jp[i]))

    finish(0)

    def halo_copy(side, other):
        return pltpu.make_async_remote_copy(
            src_ref=xs.at[0],
            dst_ref=halo.at[side],
            send_sem=halo_out.at[side],
            recv_sem=halo_in.at[side],
            device_id={"wide": other},
            device_id_type=MESH,
        )

    halo_copy(0, high_line).start()
    halo_copy(1, low_line).start()

    store_cells(xs[0].reshape(cells * NR, LANES), first_ref)

    loads[4].wait()
    weights = []
    for place in range(3):
        total = jnp.zeros((cells, NV), F32)
        for side in range(2):
            relative = lax.rem(face_ref[0, side] - line + 1 + lines, lines)
            total = total + jnp.where(
                relative == place, coef_ref[:, pl.ds(side * NV, NV)], 0.0
            )
        weights.append(jnp.concatenate([total, jnp.zeros((cells, LANES - NV), F32)], axis=1))

    halo_copy(0, high_line).wait_recv()
    halo_copy(1, low_line).wait_recv()

    for i in range(cells):
        coupled = (
            weights[0][i : i + 1] * halo[0, i]
            + weights[1][i : i + 1] * xs[0, i]
            + weights[2][i : i + 1] * halo[1, i]
        )
        src[i] = src[i] - coupled

    fsend[1] = deep([src[i] for i in range(cells)], suffixes)
    send_f(1)
    sweep()
    finish(1)
    store_cells(xs[1].reshape(cells * NR, LANES), second_ref)

    halo_copy(0, high_line).wait_send()
    halo_copy(1, low_line).wait_send()

    def drain(step, _):
        @pl.when(me + step < n)
        def _():
            f_copy(0, step, me + step).wait_send()
            f_copy(1, step, me + step).wait_send()

        @pl.when(me - step >= 0)
        def _():
            g_copy(0, n - step, me - step).wait_send()
            g_copy(1, n - step, me - step).wait_send()

        @pl.when((me >= 1) & (me + step < n))
        def _():
            map_copy(0, step, me + step).wait_send()

        @pl.when((me <= n - 2) & (me - step >= 0))
        def _():
            map_copy(1, n - step, me - step).wait_send()

        return 0

    lax.fori_loop(1, n, drain, 0)


def body(n, lines, rhs, pivot, upper, lower, neighbors, coupling):
    cells = rhs.shape[1]
    matrix = (LANES, 2 * LANES)
    tree = pltpu.VMEM((2 * cells - 1, *matrix), BF16)
    weight = pltpu.VMEM((cells, *matrix), BF16)
    vectors = pltpu.VMEM((cells, NR, LANES), F32)
    vmem = pl.BlockSpec(memory_space=pltpu.VMEM)
    hbm = pl.BlockSpec(memory_space=pltpu.HBM)
    dma = pltpu.SemaphoreType.DMA
    first, second = pl.pallas_call(
        functools.partial(kernel, n, lines),
        out_shape=[jax.ShapeDtypeStruct((cells, NV * NR), F32)] * 2,
        in_specs=[hbm] * 4 + [pl.BlockSpec(memory_space=pltpu.SMEM), hbm],
        out_specs=[vmem] * 2,
        scratch_shapes=[
            pltpu.VMEM((3, cells, NV * NV), BF16),
            pltpu.VMEM((cells, NV * NR), F32),
            pltpu.VMEM((cells, 2 * NV), F32),
            pltpu.VMEM((3, ROWS * cells, LANES), F32),
            pltpu.VMEM((LANES, LANES), F32),
            pltpu.VMEM((cells, LANES, LANES), BF16),
            tree,
            tree,
            weight,
            weight,
            weight,
            weight,
            weight,
            pltpu.VMEM((1, *matrix), BF16),
            pltpu.VMEM((2, PACKED, LANES), F32),
            pltpu.VMEM((n, PACKED, LANES), F32),
            pltpu.VMEM((n, *matrix), BF16),
            vectors,
            vectors,
            vectors,
            pltpu.VMEM((2, cells, NR, LANES), F32),
            pltpu.VMEM((2, cells, NR, LANES), F32),
            pltpu.VMEM((2, NR, LANES), F32),
            pltpu.VMEM((2, NR, LANES), F32),
            pltpu.VMEM((2, n, NR, LANES), F32),
            pltpu.VMEM((2, n, NR, LANES), F32),
            dma((5,)),
            dma((n,)),
            dma((n,)),
            dma((2, n)),
            dma((2, n)),
            dma((2, n)),
            dma((2, n)),
            dma((2,)),
            dma((2,)),
        ],
        compiler_params=pltpu.CompilerParams(
            collective_id=0, has_side_effects=True, vmem_limit_bytes=56 * 1024 * 1024
        ),
    )(pivot[0], upper[0], lower[0], rhs[0], neighbors, coupling[0])
    return first[None], second[None]


def solution(mesh):
    blocks = P("wide", "narrow", None)
    return jax.shard_map(
        functools.partial(body, mesh.shape["narrow"], mesh.shape["wide"]),
        mesh=mesh,
        in_specs=(blocks, blocks, blocks, blocks, P("wide", None), blocks),
        out_specs=(blocks, blocks),
        check_vma=False,
    )
```

time: 263 us -> 51.4 us (0.20)
  the two profiles are of different devices: /device:TPU:24 before, /device:TPU:2 now
where the time goes in v1:
time: 51.4 us; the launch traced here: 51.2 us
  Pallas kernels  48.5 us (94%)
  local copies, waits for them, and re-layouts  2.06 us (4%)
  between operations  0.65 us (1%)
    pallas_call x1, Pallas kernels, body(): pl.pallas_call(functools.partial(kernel, n, lines), out_shape=[jax.ShapeD...  48.5 us
    unnamed x4, local copies, waits for them, and re-layouts  2.06 us

profile of v1, /device:TPU:2, one launch (start us, length us, event | category | flops | bytes accessed | tf_op | source)
XLA Modules:
  0.0 51.2 jit_solution(7929228103180438498)
XLA Ops:
  0.6 48.5 %shard_map.77 = (f32[16,760]{1,0:T(8,128)}, f32[16,760]{1,0:T(8,128)}) custom-call(bf16[16,9025]{1,0:T(8,128)(2,1)} %bitcast.7, bf16[16,9025]{1,0:T(8,128)(2,1)} %bitcast.8, bf16[16,9025]{1,0:T(8,128)(2,1)} %bitcast.9, f32[16,760]{1,0:T(8,128)} %bitcast.10, s32[1,2]{1,0:T(1,128)} %face_ref.1, f32[16,190]{1,0:T(8,128)} %bitcast.13), custom_call_target="tpu_custom_call" | custom-call | tf_op jit(solution)/shard_map/pallas_call | solution.py:573
  49.1 0.0 copy-start
  49.1 1.4 %copy.10 = f32[1,16,760]{2,1,0:T(8,128)} copy(f32[1,16,760]{2,1,0:T(8,128)} %bitcast.12) | data formatting | bytes 97280
  50.6 0.0 copy-done
  50.6 0.6 %copy.11 = f32[1,16,760]{2,1,0:T(8,128)} copy(f32[1,16,760]{2,1,0:T(8,128)S(1)} %bitcast.11) | data formatting | bytes 97280
Async XLA Ops:
  49.1 1.4 %copy-start = (f32[16,760]{1,0:T(8,128)S(1)}, f32[16,760]{1,0:T(8,128)}, u32[]{:S(2)}) copy-start(f32[16,760]{1,0:T(8,128)} %get-tuple-element.5) | copy-start | bytes 145924

commit v2 on v1

--- a/solution.py
+++ b/solution.py
@@ -143,18 +143,20 @@
     pivot,
     tn,
     tb,
-    qw,
     ew,
     kw,
     jw,
     jp,
     hw,
+    hsum,
+    rho,
     maps,
     came,
+    answers,
+    answered,
     phi,
     src,
     zs,
-    us,
     xs,
     halo,
     fsend,
@@ -164,6 +166,8 @@
     load_sem,
     map_out,
     map_in,
+    answer_out,
+    answer_in,
     f_out,
     f_in,
     g_out,
@@ -188,6 +192,7 @@
 
     fcame[...] = jnp.zeros_like(fcame)
     gcame[...] = jnp.zeros_like(gcame)
+    answered[...] = jnp.zeros_like(answered)
 
     barrier = pltpu.get_barrier_semaphore()
 
@@ -212,12 +217,14 @@
     lax.fori_loop(0, 2 * cells - 1, clear_nodes, 0)
 
     def clear(i, _):
-        for ref in (qw, ew, kw, jw, jp):
+        for ref in (ew, kw, jw, jp):
             ref[i, pl.ds(ROWS, LANES - ROWS), :] = tail
         return 0
 
     lax.fori_loop(0, cells, clear, 0)
     hw[0, pl.ds(ROWS, LANES - ROWS), :] = tail
+    for i in range(3):
+        rho[i, pl.ds(ROWS, LANES - ROWS), :] = tail
 
     def clear_phi(i, _):
         phi[i] = jnp.zeros((LANES, 2 * LANES), BF16)
@@ -300,8 +307,9 @@
         return 0
 
     lax.fori_loop(1, n, send_maps, 0)
-    put(tn, cells + last, forward)
-    put(tb, cells + last, backward)
+    whole = cells + last
+    put(tn, whole, forward)
+    put(tb, whole, backward)
 
     def offset_copy(source, target_ref, turn, slot, out, arrived, target):
         return pltpu.make_async_remote_copy(
@@ -368,128 +376,181 @@
         ref, index = place
         return folded(dot(stacked_vector(vector), ref[index]))
 
-    def first_n(m):
-        return (tn, node(m, cells, 0)) if m and low_bit(m) == m else (kw, m)
-
-    def last_n(m):
-        return (tn, node(m, cells, cells - m)) if low_bit(m) == m else (qw, m)
-
-    def last_b(m):
-        return (tb, node(m, cells, cells - m)) if m and low_bit(m) == m else (jw, m)
-
-    def first_b(m):
-        return (tb, node(m, cells, 0)) if low_bit(m) == m else (ew, m)
+    def forward_node(size, first):
+        return tn, node(size, cells, first)
+
+    def backward_node(size, first):
+        return tb, node(size, cells, cells - first - size)
+
+    def climb(source, at, whole):
+        sums, source = {}, list(source)
+        for p in range(0, cells, 2):
+            source[p + 1] = source[p + 1] + by(source[p], at(1, p))
+        for p in range(0, cells, 2):
+            sums[2, p] = by(source[p + 1], at(1, p + 1))
+        size = 2
+        while size < cells // 2 or (whole and size < cells):
+            for p in range(0, cells, 2 * size):
+                sums[2 * size, p] = sums[size, p + size] + by(sums[size, p], at(size, p + size))
+            size *= 2
+        return source, sums
+
+    def descend(source, sums, at):
+        entering = {0: None}
+        size = cells // 2
+        while size >= 2:
+            for p in range(0, cells, 2 * size):
+                after = sums[size, p]
+                if entering[p] is not None:
+                    after = after + by(entering[p], at(size, p))
+                entering[p + size] = after
+            size //= 2
+        values = list(source)
+        for p in range(0, cells, 2):
+            if entering[p] is not None:
+                values[p] = values[p] + entering[p]
+                values[p + 1] = values[p + 1] + by(entering[p], at(1, p))
+        return values
 
     row = lax.broadcasted_iota(jnp.int32, (ROWS, LANES), 0)
     column = lax.broadcasted_iota(jnp.int32, (ROWS, LANES), 1)
     unit = jnp.where((row == column) & (row < NV), 1.0, 0.0).astype(F32)
     put(kw, 0, unit)
-    put(jw, 0, unit)
+    put(jw, cells - 1, unit)
+    ew[0] = tb[0]
+    hsum[...] = jnp.zeros_like(hsum)
+    came[0] = jnp.zeros_like(came[0])
+
+    @pl.when(me >= 1)
+    def _():
+        put(phi, 1, unit)
+
+    @pl.when(me <= n - 2)
+    def _():
+        put(phi, n - 1, unit)
+
+    def start(turn):
+        source, sums = climb([src[i] for i in range(cells)], forward_node, True)
+        leaving = sums[cells, 0]
+        fsend[turn] = leaving
+        send_f(turn)
+        for i, value in enumerate(descend(source, sums, forward_node)):
+            zs[i] = value
+        return leaving
 
     loads[3].wait()
     blocks = load_cells(rhs_ref, pad)
     for i in range(cells):
         src[i] = blocks[i * NR : (i + 1) * NR]
-
-    mixed = [m for m in range(1, cells) if low_bit(m) != m]
-    for m in mixed:
-        size = low_bit(m)
-        at_end = node(size, cells, m - size)
-        at_start = node(size, cells, cells - m)
-        put(qw, m, multiply(left_of((tn, at_start)), right_of(last_n(m - size))))
-        put(ew, m, multiply(left_of((tb, at_end)), right_of(first_b(m - size))))
-
-    suffixes = [last_n(cells - i) for i in range(cells)]
-    prefixes = [first_b(i + 1) for i in range(cells)]
-
-    fsend[0] = deep([src[i] for i in range(cells)], suffixes)
-    send_f(0)
-
-    for m in mixed:
-        size = low_bit(m)
-        at_end = node(size, cells, m - size)
-        at_start = node(size, cells, cells - m)
-        put(kw, m, multiply(left_of(first_n(m - size)), right_of((tn, at_end))))
-        put(jw, m, multiply(left_of(last_b(m - size)), right_of((tb, at_start))))
-
-    response = multiply(
-        jnp.concatenate([left_of(first_n(i)) for i in range(cells)], axis=1),
-        jnp.concatenate([right_of(first_b(i + 1)) for i in range(cells)], axis=0),
-    )
-    put(hw, 0, response)
-    for i in range(cells):
+    start(0)
+
+    from_before = jnp.maximum(me - 1, 0)
+    from_after = jnp.maximum(n - 2 - me, 0)
+
+    def with_pivot(i):
         exact = pivot[i]
-        put(jp, i, dot(left_of(last_b(cells - 1 - i)), jnp.concatenate([exact, exact], axis=0)))
-
-    def sweep():
-        def forward(i, z):
-            z = src[i] + by(z, (tn, i - 1))
-            zs[i] = z
-            return z
-
-        zs[0] = src[0]
-        lax.fori_loop(1, cells, forward, src[0])
-
-    sweep()
-
-    @pl.when(me >= 1)
-    def _():
-        put(phi, 1, unit)
-
-    @pl.when(me <= n - 2)
-    def _():
-        put(phi, n - 1, unit)
-
-    def extend(slot, towards):
+        put(jp, i, dot(left_of((jw, i)), jnp.concatenate([exact, exact], axis=0)))
+
+    def tables(step, _):
+        before = step <= from_before
+        after = step - from_before
+        arrived = before | (after <= from_after)
+        slot = jnp.where(before, step, jnp.where(arrived, n - after, 0))
+        towards = jnp.where(before, step + 1, jnp.where(arrived, n - after - 1, n))
+
+        @pl.when(arrived)
+        def _():
+            map_copy(0, slot, me).wait_recv()
+
         high, low = parts(unpacked(came[slot]))
-        put(phi, towards, multiply(jnp.concatenate([high, low], axis=1), right_of((phi, slot))))
-
-    def chain(step, _):
-        @pl.when(step <= me - 1)
-        def _():
-            map_copy(0, step, me).wait_recv()
-            extend(step, step + 1)
-
-        @pl.when(step <= n - 2 - me)
-        def _():
-            map_copy(1, n - step, me).wait_recv()
-            extend(n - step, n - step - 1)
-
-        return 0
-
-    lax.fori_loop(1, n - 1, chain, 0)
+        chained = multiply(jnp.concatenate([high, low], axis=1), right_of((phi, slot)))
+        back = cells - 1 - step
+        k = multiply(left_of((kw, step - 1)), right_of((tn, step - 1)))
+        e = multiply(left_of((tb, step)), right_of((ew, step - 1)))
+        j = multiply(left_of((jw, back + 1)), right_of((tb, back + 1)))
+        h = multiply(left_of((kw, step - 1)), right_of((ew, step - 1)))
+        with_pivot(back + 1)
+        put(phi, towards, chained)
+        put(kw, step, k)
+        put(ew, step, e)
+        put(jw, back, j)
+        hsum[...] += h
+        return 0
+
+    lax.fori_loop(1, cells, tables, 0)
+    with_pivot(0)
+    put(hw, 0, hsum[...] + multiply(left_of((kw, cells - 1)), right_of((ew, cells - 1))))
 
     between = [(phi, k) for k in range(n)]
 
-    def finish(turn):
-        alone = deep([zs[i] for i in range(cells)], prefixes)
-        wait_f(turn)
-        entering = deep([fcame[turn, k] for k in range(n)], between)
-        left = stacked_vector(entering)
-        gsend[turn] = alone + folded(dot(left, hw[0]))
-        send_g(turn)
-        for i in range(cells):
-            ref, index = first_n(i)
-            zs[i] = zs[i] + folded(dot(left, ref[index]))
-        us[cells - 1] = zs[cells - 1]
-
-        def backward(i, u):
-            back = cells - 1 - i
-            u = zs[back] + by(u, (tb, back + 1))
-            us[back] = u
-            return u
-
-        lax.fori_loop(1, cells, backward, zs[cells - 1])
-        for i in range(cells):
-            product = dot(stacked_vector(us[i]), pivot[i])
+    def answer_copy(slot, target):
+        return pltpu.make_async_remote_copy(
+            src_ref=answers.at[slot],
+            dst_ref=answered.at[slot],
+            send_sem=answer_out.at[slot],
+            recv_sem=answer_in.at[slot],
+            device_id={"narrow": target},
+            device_id_type=MESH,
+        )
+
+    def send_answers():
+        high_low = jnp.concatenate([left_of((phi, k)) for k in range(1, n)], axis=0)
+        products = multiply(high_low, right_of((hw, 0)))
+        for k in range(1, n):
+            answers[n - k] = packed(products[(k - 1) * ROWS : k * ROWS])
+
+        def send(step, _):
+            answer_copy(n - step, me - step).start()
+            return 0
+
+        lax.fori_loop(1, me + 1, send, 0)
+
+    def take_answers():
+        def wait(step, _):
+            answer_copy(n - step, me).wait_recv()
+            return 0
+
+        lax.fori_loop(1, n - me, wait, 0)
+        left = []
+        for k in range(1, n):
+            high, low = parts(unpacked(answered[k]))
+            left += [high, low]
+        put(
+            rho,
+            0,
+            multiply(
+                jnp.concatenate(left, axis=1),
+                jnp.concatenate([right_of((phi, k)) for k in range(1, n)], axis=0),
+            ),
+        )
+        put(rho, 1, multiply(left_of((rho, 0)), right_of((tb, whole))))
+        put(rho, 2, multiply(left_of((tn, whole)), right_of((rho, 0))))
+
+    def inside(turn, left):
+        z = [zs[i] + folded(dot(left, kw[i])) for i in range(cells)]
+        source, sums = climb(z[::-1], backward_node, False)
+        for p, u in enumerate(descend(source, sums, backward_node)):
+            i = cells - 1 - p
+            product = dot(stacked_vector(u), pivot[i])
             xs[turn, i] = product[:NR] + product[NR:]
-        wait_g(turn)
-        entering = deep([gcame[turn, k] for k in range(n)], between)
+
+    def complete(turn, entering):
         left = stacked_vector(entering)
         for i in range(cells):
             xs[turn, i] = xs[turn, i] + folded(dot(left, jp[i]))
 
-    finish(0)
+    def backward_alone():
+        return deep([zs[i] for i in range(cells)], [(ew, i) for i in range(cells)])
+
+    alone = backward_alone()
+    wait_f(0)
+    left = stacked_vector(deep([fcame[0, k] for k in range(n)], between))
+    gsend[0] = alone + folded(dot(left, hw[0]))
+    send_g(0)
+    send_answers()
+    inside(0, left)
+    wait_g(0)
+    complete(0, deep([gcame[0, k] for k in range(n)], between))
 
     def halo_copy(side, other):
         return pltpu.make_async_remote_copy(
@@ -517,6 +578,8 @@
             )
         weights.append(jnp.concatenate([total, jnp.zeros((cells, LANES - NV), F32)], axis=1))
 
+    take_answers()
+
     halo_copy(0, high_line).wait_recv()
     halo_copy(1, low_line).wait_recv()
 
@@ -528,10 +591,15 @@
         )
         src[i] = src[i] - coupled
 
-    fsend[1] = deep([src[i] for i in range(cells)], suffixes)
-    send_f(1)
-    sweep()
-    finish(1)
+    leaving = start(1)
+    gsend[1] = backward_alone() + by(leaving, (rho, 1))
+    send_g(1)
+    wait_f(1)
+    left = stacked_vector(deep([fcame[1, k] for k in range(n)], between))
+    inside(1, left)
+    back = by(leaving, (rho, 0)) + folded(dot(left, rho[2]))
+    wait_g(1)
+    complete(1, back + deep([gcame[1, k] for k in range(n)], between))
     store_cells(xs[1].reshape(cells * NR, LANES), second_ref)
 
     halo_copy(0, high_line).wait_send()
@@ -547,6 +615,7 @@
         def _():
             g_copy(0, n - step, me - step).wait_send()
             g_copy(1, n - step, me - step).wait_send()
+            answer_copy(n - step, me - step).wait_send()
 
         @pl.when((me >= 1) & (me + step < n))
         def _():
@@ -588,12 +657,14 @@
             weight,
             weight,
             weight,
-            weight,
             pltpu.VMEM((1, *matrix), BF16),
+            pltpu.VMEM((ROWS, LANES), F32),
+            pltpu.VMEM((3, *matrix), BF16),
             pltpu.VMEM((2, PACKED, LANES), F32),
             pltpu.VMEM((n, PACKED, LANES), F32),
-            pltpu.VMEM((n, *matrix), BF16),
-            vectors,
+            pltpu.VMEM((n, PACKED, LANES), F32),
+            pltpu.VMEM((n, PACKED, LANES), F32),
+            pltpu.VMEM((n + 1, *matrix), BF16),
             vectors,
             vectors,
             pltpu.VMEM((2, cells, NR, LANES), F32),
@@ -603,6 +674,8 @@
             pltpu.VMEM((2, n, NR, LANES), F32),
             pltpu.VMEM((2, n, NR, LANES), F32),
             dma((5,)),
+            dma((n,)),
+            dma((n,)),
             dma((n,)),
             dma((n,)),
             dma((2, n)),

time: 51.4 us -> 48.6 us (0.946)
  the two profiles are of different devices: /device:TPU:2 before, /device:TPU:24 now
where the time goes in v2:
time: 48.6 us; the launch traced here: 48.4 us
  Pallas kernels  45.7 us (94%)
  local copies, waits for them, and re-layouts  2.06 us (4%)
  between operations  0.65 us (1%)
    pallas_call x1, Pallas kernels, body(): pl.pallas_call(functools.partial(kernel, n, lines), out_shape=[jax.ShapeD...  45.7 us
    unnamed x4, local copies, waits for them, and re-layouts  2.06 us

profile of v2, /device:TPU:24, one launch (start us, length us, event | category | flops | bytes accessed | tf_op | source)
XLA Modules:
  0.0 48.4 jit_solution(12826244473974875383)
XLA Ops:
  0.6 45.7 %shard_map.77 = (f32[16,760]{1,0:T(8,128)}, f32[16,760]{1,0:T(8,128)}) custom-call(bf16[16,9025]{1,0:T(8,128)(2,1)} %bitcast.7, bf16[16,9025]{1,0:T(8,128)(2,1)} %bitcast.8, bf16[16,9025]{1,0:T(8,128)(2,1)} %bitcast.9, f32[16,760]{1,0:T(8,128)} %bitcast.10, s32[1,2]{1,0:T(1,128)} %face_ref.1, f32[16,190]{1,0:T(8,128)} %bitcast.13), custom_call_target="tpu_custom_call" | custom-call | tf_op jit(solution)/shard_map/pallas_call | solution.py:642
  46.3 0.0 copy-start
  46.3 1.4 %copy.10 = f32[1,16,760]{2,1,0:T(8,128)} copy(f32[1,16,760]{2,1,0:T(8,128)} %bitcast.12) | data formatting | bytes 97280
  47.8 0.0 copy-done
  47.8 0.6 %copy.11 = f32[1,16,760]{2,1,0:T(8,128)} copy(f32[1,16,760]{2,1,0:T(8,128)S(1)} %bitcast.11) | data formatting | bytes 97280
Async XLA Ops:
  46.3 1.4 %copy-start = (f32[16,760]{1,0:T(8,128)S(1)}, f32[16,760]{1,0:T(8,128)}, u32[]{:S(2)}) copy-start(f32[16,760]{1,0:T(8,128)} %get-tuple-element.5) | copy-start | bytes 145924

commit v3 on v2

--- a/solution.py
+++ b/solution.py
@@ -114,6 +114,10 @@
         first = block * LANES
         wide = min(LANES, width - first)
         flat_ref[:, pl.ds(first, wide)] = turned[block * 16 : block * 16 + cells, :wide]
+
+
+def far_first(n):
+    return sorted(range(1, n), key=lambda step: -sum(min(d, 4 - d) for d in (step % 4, step // 4 % 4)))
 
 
 def low_bit(m):
@@ -273,9 +277,8 @@
         return 0
 
     last = cells - 2
-    grouped = (cells - 4) // together
-    lax.fori_loop(0, grouped, join_group, 0)
-    for place in range(grouped * together, last):
+    lax.fori_loop(0, 2, join_group, 0)
+    for place in range(2 * together, last):
         forward, backward = join(place)
         put(tn, cells + place, forward)
         put(tb, cells + place, backward)
@@ -328,44 +331,32 @@
         return offset_copy(gsend, gcame, turn, slot, g_out, g_in, target)
 
     def send_f(turn):
-        def send(step, _):
+        for step in far_first(n):
+
             @pl.when(me + step < n)
             def _():
                 f_copy(turn, step, me + step).start()
 
-            return 0
-
-        lax.fori_loop(1, n, send, 0)
-
     def send_g(turn):
-        def send(step, _):
+        for step in far_first(n):
+
             @pl.when(me - step >= 0)
             def _():
                 g_copy(turn, n - step, me - step).start()
 
-            return 0
-
-        lax.fori_loop(1, n, send, 0)
-
     def wait_f(turn):
-        def wait(step, _):
+        for step in range(1, n):
+
             @pl.when(step <= me)
             def _():
                 f_copy(turn, step, me).wait_recv()
 
-            return 0
-
-        lax.fori_loop(1, n, wait, 0)
-
     def wait_g(turn):
-        def wait(step, _):
+        for step in range(1, n):
+
             @pl.when(me + step < n)
             def _():
                 g_copy(turn, n - step, me).wait_recv()
-
-            return 0
-
-        lax.fori_loop(1, n, wait, 0)
 
     def deep(vectors, weights):
         left = jnp.concatenate([stacked_vector(v) for v in vectors], axis=1)
@@ -578,6 +569,26 @@
             )
         weights.append(jnp.concatenate([total, jnp.zeros((cells, LANES - NV), F32)], axis=1))
 
+    def drain(step, _):
+        @pl.when(me + step < n)
+        def _():
+            f_copy(0, step, me + step).wait_send()
+
+        @pl.when(me - step >= 0)
+        def _():
+            g_copy(0, n - step, me - step).wait_send()
+
+        @pl.when((me >= 1) & (me + step < n))
+        def _():
+            map_copy(0, step, me + step).wait_send()
+
+        @pl.when((me <= n - 2) & (me - step >= 0))
+        def _():
+            map_copy(1, n - step, me - step).wait_send()
+
+        return 0
+
+    lax.fori_loop(1, n, drain, 0)
     take_answers()
 
     halo_copy(0, high_line).wait_recv()
@@ -598,36 +609,25 @@
     left = stacked_vector(deep([fcame[1, k] for k in range(n)], between))
     inside(1, left)
     back = by(leaving, (rho, 0)) + folded(dot(left, rho[2]))
+    halo_copy(0, high_line).wait_send()
+    halo_copy(1, low_line).wait_send()
+
+    def drain_last(step, _):
+        @pl.when(me + step < n)
+        def _():
+            f_copy(1, step, me + step).wait_send()
+
+        @pl.when(me - step >= 0)
+        def _():
+            g_copy(1, n - step, me - step).wait_send()
+            answer_copy(n - step, me - step).wait_send()
+
+        return 0
+
+    lax.fori_loop(1, n, drain_last, 0)
     wait_g(1)
     complete(1, back + deep([gcame[1, k] for k in range(n)], between))
     store_cells(xs[1].reshape(cells * NR, LANES), second_ref)
-
-    halo_copy(0, high_line).wait_send()
-    halo_copy(1, low_line).wait_send()
-
-    def drain(step, _):
-        @pl.when(me + step < n)
-        def _():
-            f_copy(0, step, me + step).wait_send()
-            f_copy(1, step, me + step).wait_send()
-
-        @pl.when(me - step >= 0)
-        def _():
-            g_copy(0, n - step, me - step).wait_send()
-            g_copy(1, n - step, me - step).wait_send()
-            answer_copy(n - step, me - step).wait_send()
-
-        @pl.when((me >= 1) & (me + step < n))
-        def _():
-            map_copy(0, step, me + step).wait_send()
-
-        @pl.when((me <= n - 2) & (me - step >= 0))
-        def _():
-            map_copy(1, n - step, me - step).wait_send()
-
-        return 0
-
-    lax.fori_loop(1, n, drain, 0)
 
 
 def body(n, lines, rhs, pivot, upper, lower, neighbors, coupling):
@@ -639,9 +639,13 @@
     vmem = pl.BlockSpec(memory_space=pltpu.VMEM)
     hbm = pl.BlockSpec(memory_space=pltpu.HBM)
     dma = pltpu.SemaphoreType.DMA
+
+    def in_hbm(x):
+        return pltpu.with_memory_space_constraint(x, pltpu.HBM)
+
     first, second = pl.pallas_call(
         functools.partial(kernel, n, lines),
-        out_shape=[jax.ShapeDtypeStruct((cells, NV * NR), F32)] * 2,
+        out_shape=[pltpu.VMEM((cells, NV * NR), F32)] * 2,
         in_specs=[hbm] * 4 + [pl.BlockSpec(memory_space=pltpu.SMEM), hbm],
         out_specs=[vmem] * 2,
         scratch_shapes=[
@@ -686,9 +690,9 @@
             dma((2,)),
         ],
         compiler_params=pltpu.CompilerParams(
-            collective_id=0, has_side_effects=True, vmem_limit_bytes=56 * 1024 * 1024
+            collective_id=0, has_side_effects=True, vmem_limit_bytes=40 * 1024 * 1024
         ),
-    )(pivot[0], upper[0], lower[0], rhs[0], neighbors, coupling[0])
+    )(*(in_hbm(x) for x in (pivot[0], upper[0], lower[0], rhs[0], neighbors, coupling[0])))
     return first[None], second[None]
 
 

time: 48.6 us -> 46.2 us (0.951)
  Pallas kernels: 45.7 us -> 44.1 us
  local copies, waits for them, and re-layouts: 2.06 us -> 1.24 us
    pallas_call x1, Pallas kernels: 45.7 us -> 44.1 us  [body(): pl.pallas_call(functools.partial(kernel, n, lines), out_shape=[pltpu.VMEM...]
    unnamed x4 -> x2, local copies, waits for them, and re-layouts: 2.06 us -> 1.24 us
where the time goes in v3:
time: 46.2 us; the launch traced here: 46 us
  Pallas kernels  44.1 us (95%)
  local copies, waits for them, and re-layouts  1.24 us (3%)
  between operations  0.64 us (1%)
    pallas_call x1, Pallas kernels, body(): pl.pallas_call(functools.partial(kernel, n, lines), out_shape=[pltpu.VMEM...  44.1 us
    unnamed x2, local copies, waits for them, and re-layouts  1.24 us

profile of v3, /device:TPU:24, one launch (start us, length us, event | category | flops | bytes accessed | tf_op | source)
XLA Modules:
  0.0 46.0 jit_solution(9226758156269864060)
XLA Ops:
  0.6 44.1 %shard_map.77 = (f32[16,760]{1,0:T(8,128)S(1)}, f32[16,760]{1,0:T(8,128)S(1)}) custom-call(bf16[16,9025]{1,0:T(8,128)(2,1)} %bitcast.9, bf16[16,9025]{1,0:T(8,128)(2,1)} %bitcast.10, bf16[16,9025]{1,0:T(8,128)(2,1)} %bitcast.11, f32[16,760]{1,0:T(8,128)} %bitcast.12, s32[1,2]{1,0:T(1,128)} %face_ref.1, f32[16,190]{1,0:T(8,128)} %bitcast.13), custom_call_target="tpu_custom_call" | custom-call | tf_op jit(solution)/shard_map/pallas_call | solution.py:646
  44.8 0.6 %copy.10 = f32[1,16,760]{2,1,0:T(8,128)} copy(f32[1,16,760]{2,1,0:T(8,128)S(1)} %bitcast.8) | data formatting | bytes 97280
  45.4 0.6 %copy.11 = f32[1,16,760]{2,1,0:T(8,128)} copy(f32[1,16,760]{2,1,0:T(8,128)S(1)} %bitcast.7) | data formatting | bytes 97280

commit v4 on v3

--- a/solution.py
+++ b/solution.py
@@ -114,6 +114,11 @@
         first = block * LANES
         wide = min(LANES, width - first)
         flat_ref[:, pl.ds(first, wide)] = turned[block * 16 : block * 16 + cells, :wide]
+
+
+def mixed_near_first(n):
+    early = {4: 1.5, 8: 4.5, 12: 8.5}
+    return sorted(range(1, n), key=lambda step: early.get(step, step))
 
 
 def far_first(n):
@@ -239,46 +244,31 @@
     for number in range(3):
         loads[number].wait()
         for row in range(NV):
-            slab[number, pl.ds(row * cells, cells), pl.ds(0, NV)] = flat[
+            slab[number, pl.ds(row * (cells + 1), cells), pl.ds(0, NV)] = flat[
                 number, :, pl.ds(row * NV, NV)
             ].astype(F32)
 
     no_rows = jnp.zeros((LANES - ROWS, LANES), BF16)
-    together = 4
-
-    def multiply_blocks(group, _):
-        for member in range(together):
-            i = group * together + member
-            p, u, l = (
-                slab[number, pl.ds(i, ROWS, stride=cells), :] for number in range(3)
-            )
-            p16 = p.astype(BF16)
-            pivot[i] = jnp.concatenate([p16, no_rows], axis=0)
-            right = jnp.concatenate([(-u).astype(BF16), (-l).astype(BF16)], axis=1)
-            right = jnp.concatenate([right, tail], axis=0)
-            both = dot(p16, right)
-            put(tn, i, both[:, :LANES])
-            put(tb, i, both[:, LANES:])
-        return 0
-
-    lax.fori_loop(0, cells // together, multiply_blocks, 0)
+
+    for i in range(cells):
+        p, u, l = (
+            slab[number, pl.ds(i, ROWS, stride=cells + 1), :] for number in range(3)
+        )
+        p16 = p.astype(BF16)
+        pivot[i] = jnp.concatenate([p16, no_rows], axis=0)
+        right = jnp.concatenate([(-u).astype(BF16), (-l).astype(BF16)], axis=1)
+        right = jnp.concatenate([right, tail], axis=0)
+        both = dot(p16, right)
+        put(tn, i, both[:, :LANES])
+        put(tb, i, both[:, LANES:])
 
     def join(place):
         forward = multiply(left_of((tn, 2 * place)), right_of((tn, 2 * place + 1)))
         backward = multiply(left_of((tb, 2 * place + 1)), right_of((tb, 2 * place)))
         return forward, backward
 
-    def join_group(group, _):
-        for member in range(together):
-            place = group * together + member
-            forward, backward = join(place)
-            put(tn, cells + place, forward)
-            put(tb, cells + place, backward)
-        return 0
-
     last = cells - 2
-    lax.fori_loop(0, 2, join_group, 0)
-    for place in range(2 * together, last):
+    for place in range(last):
         forward, backward = join(place)
         put(tn, cells + place, forward)
         put(tb, cells + place, backward)
@@ -298,7 +288,8 @@
             device_id_type=MESH,
         )
 
-    def send_maps(step, _):
+    for step in mixed_near_first(n):
+
         @pl.when((me >= 1) & (me + step < n))
         def _():
             map_copy(0, step, me + step).start()
@@ -307,9 +298,6 @@
         def _():
             map_copy(1, n - step, me - step).start()
 
-        return 0
-
-    lax.fori_loop(1, n, send_maps, 0)
     whole = cells + last
     put(tn, whole, forward)
     put(tb, whole, backward)
@@ -652,7 +640,7 @@
             pltpu.VMEM((3, cells, NV * NV), BF16),
             pltpu.VMEM((cells, NV * NR), F32),
             pltpu.VMEM((cells, 2 * NV), F32),
-            pltpu.VMEM((3, ROWS * cells, LANES), F32),
+            pltpu.VMEM((3, ROWS * (cells + 1), LANES), F32),
             pltpu.VMEM((LANES, LANES), F32),
             pltpu.VMEM((cells, LANES, LANES), BF16),
             tree,

time: 46.2 us -> 44.2 us (0.957)
  Pallas kernels: 44.1 us -> 42.1 us
    pallas_call x1, Pallas kernels: 44.1 us -> 42.1 us  [body(): pl.pallas_call(functools.partial(kernel, n, lines), out_shape=[pltpu.VMEM...]
where the time goes in v4:
time: 44.2 us; the launch traced here: 44 us
  Pallas kernels  42.1 us (95%)
  local copies, waits for them, and re-layouts  1.24 us (3%)
  between operations  0.64 us (1%)
    pallas_call x1, Pallas kernels, body(): pl.pallas_call(functools.partial(kernel, n, lines), out_shape=[pltpu.VMEM...  42.1 us
    unnamed x2, local copies, waits for them, and re-layouts  1.24 us

profile of v4, /device:TPU:24, one launch (start us, length us, event | category | flops | bytes accessed | tf_op | source)
XLA Modules:
  0.0 44.0 jit_solution(6590975005054708205)
XLA Ops:
  0.6 42.1 %shard_map.77 = (f32[16,760]{1,0:T(8,128)S(1)}, f32[16,760]{1,0:T(8,128)S(1)}) custom-call(bf16[16,9025]{1,0:T(8,128)(2,1)} %bitcast.9, bf16[16,9025]{1,0:T(8,128)(2,1)} %bitcast.10, bf16[16,9025]{1,0:T(8,128)(2,1)} %bitcast.11, f32[16,760]{1,0:T(8,128)} %bitcast.12, s32[1,2]{1,0:T(1,128)} %face_ref.1, f32[16,190]{1,0:T(8,128)} %bitcast.13), custom_call_target="tpu_custom_call" | custom-call | tf_op jit(solution)/shard_map/pallas_call | solution.py:634
  42.8 0.6 %copy.10 = f32[1,16,760]{2,1,0:T(8,128)} copy(f32[1,16,760]{2,1,0:T(8,128)S(1)} %bitcast.8) | data formatting | bytes 97280
  43.4 0.6 %copy.11 = f32[1,16,760]{2,1,0:T(8,128)} copy(f32[1,16,760]{2,1,0:T(8,128)S(1)} %bitcast.7) | data formatting | bytes 97280

commit v5 on v4

--- a/solution.py
+++ b/solution.py
@@ -152,6 +152,7 @@
     pivot,
     tn,
     tb,
+    qw,
     ew,
     kw,
     jw,
@@ -226,7 +227,7 @@
     lax.fori_loop(0, 2 * cells - 1, clear_nodes, 0)
 
     def clear(i, _):
-        for ref in (ew, kw, jw, jp):
+        for ref in (qw, ew, kw, jw, jp):
             ref[i, pl.ds(ROWS, LANES - ROWS), :] = tail
         return 0
 
@@ -262,19 +263,12 @@
         put(tn, i, both[:, :LANES])
         put(tb, i, both[:, LANES:])
 
-    def join(place):
-        forward = multiply(left_of((tn, 2 * place)), right_of((tn, 2 * place + 1)))
-        backward = multiply(left_of((tb, 2 * place + 1)), right_of((tb, 2 * place)))
-        return forward, backward
-
     last = cells - 2
+    whole = cells + last
     for place in range(last):
-        forward, backward = join(place)
-        put(tn, cells + place, forward)
-        put(tb, cells + place, backward)
-    forward, backward = join(last)
+        put(tn, cells + place, multiply(left_of((tn, 2 * place)), right_of((tn, 2 * place + 1))))
+    forward = multiply(left_of((tn, 2 * last)), right_of((tn, 2 * last + 1)))
     maps[0] = packed(forward)
-    maps[1] = packed(backward)
 
     pl.semaphore_wait(barrier, n - 1 + 2)
 
@@ -294,11 +288,16 @@
         def _():
             map_copy(0, step, me + step).start()
 
+    for place in range(last):
+        put(tb, cells + place, multiply(left_of((tb, 2 * place + 1)), right_of((tb, 2 * place))))
+    backward = multiply(left_of((tb, 2 * last + 1)), right_of((tb, 2 * last)))
+    maps[1] = packed(backward)
+    for step in mixed_near_first(n):
+
         @pl.when((me <= n - 2) & (me - step >= 0))
         def _():
             map_copy(1, n - step, me - step).start()
 
-    whole = cells + last
     put(tn, whole, forward)
     put(tb, whole, backward)
 
@@ -408,20 +407,18 @@
     def _():
         put(phi, n - 1, unit)
 
-    def start(turn):
-        source, sums = climb([src[i] for i in range(cells)], forward_node, True)
-        leaving = sums[cells, 0]
-        fsend[turn] = leaving
-        send_f(turn)
+    def keep_alone(source, sums):
         for i, value in enumerate(descend(source, sums, forward_node)):
             zs[i] = value
-        return leaving
 
     loads[3].wait()
     blocks = load_cells(rhs_ref, pad)
     for i in range(cells):
         src[i] = blocks[i * NR : (i + 1) * NR]
-    start(0)
+    source, sums = climb([src[i] for i in range(cells)], forward_node, True)
+    fsend[0] = sums[cells, 0]
+    send_f(0)
+    keep_alone(source, sums)
 
     from_before = jnp.maximum(me - 1, 0)
     from_after = jnp.maximum(n - 2 - me, 0)
@@ -430,19 +427,20 @@
         exact = pivot[i]
         put(jp, i, dot(left_of((jw, i)), jnp.concatenate([exact, exact], axis=0)))
 
+    def extended(slot):
+        high, low = parts(unpacked(came[slot]))
+        return multiply(jnp.concatenate([high, low], axis=1), right_of((phi, slot)))
+
     def tables(step, _):
-        before = step <= from_before
-        after = step - from_before
-        arrived = before | (after <= from_after)
-        slot = jnp.where(before, step, jnp.where(arrived, n - after, 0))
-        towards = jnp.where(before, step + 1, jnp.where(arrived, n - after - 1, n))
+        arrived = step <= from_before
+        slot = jnp.where(arrived, step, 0)
+        towards = jnp.where(arrived, step + 1, n)
 
         @pl.when(arrived)
         def _():
             map_copy(0, slot, me).wait_recv()
 
-        high, low = parts(unpacked(came[slot]))
-        chained = multiply(jnp.concatenate([high, low], axis=1), right_of((phi, slot)))
+        chained = extended(slot)
         back = cells - 1 - step
         k = multiply(left_of((kw, step - 1)), right_of((tn, step - 1)))
         e = multiply(left_of((tb, step)), right_of((ew, step - 1)))
@@ -528,6 +526,14 @@
     send_g(0)
     send_answers()
     inside(0, left)
+
+    def chain_back(step, _):
+        slot = n - step
+        map_copy(1, slot, me).wait_recv()
+        put(phi, slot - 1, extended(slot))
+        return 0
+
+    lax.fori_loop(1, from_after + 1, chain_back, 0)
     wait_g(0)
     complete(0, deep([gcame[0, k] for k in range(n)], between))
 
@@ -579,6 +585,15 @@
     lax.fori_loop(1, n, drain, 0)
     take_answers()
 
+    def last_n(m):
+        return (tn, node(m, cells, cells - m)) if low_bit(m) == m else (qw, m)
+
+    for m in range(1, cells):
+        size = low_bit(m)
+        if size != m:
+            first = node(size, cells, cells - m)
+            put(qw, m, multiply(left_of((tn, first)), right_of(last_n(m - size))))
+
     halo_copy(0, high_line).wait_recv()
     halo_copy(1, low_line).wait_recv()
 
@@ -590,7 +605,10 @@
         )
         src[i] = src[i] - coupled
 
-    leaving = start(1)
+    leaving = deep([src[i] for i in range(cells)], [last_n(cells - i) for i in range(cells)])
+    fsend[1] = leaving
+    send_f(1)
+    keep_alone(*climb([src[i] for i in range(cells)], forward_node, False))
     gsend[1] = backward_alone() + by(leaving, (rho, 1))
     send_g(1)
     wait_f(1)
@@ -645,6 +663,7 @@
             pltpu.VMEM((cells, LANES, LANES), BF16),
             tree,
             tree,
+            weight,
             weight,
             weight,
             weight,

time: 44.2 us -> 42.2 us (0.955)
  Pallas kernels: 42.1 us -> 39.9 us
    pallas_call x1, Pallas kernels: 42.1 us -> 39.9 us  [body(): pl.pallas_call(functools.partial(kernel, n, lines), out_shape=[pltpu.VMEM...]
where the time goes in v5:
time: 42.2 us; the launch traced here: 41.8 us
  Pallas kernels  39.9 us (95%)
  local copies, waits for them, and re-layouts  1.24 us (3%)
  between operations  0.64 us (2%)
    pallas_call x1, Pallas kernels, body(): pl.pallas_call(functools.partial(kernel, n, lines), out_shape=[pltpu.VMEM...  39.9 us
    unnamed x2, local copies, waits for them, and re-layouts  1.24 us

profile of v5, /device:TPU:24, one launch (start us, length us, event | category | flops | bytes accessed | tf_op | source)
XLA Modules:
  0.0 41.8 jit_solution(4267057817040302778)
XLA Ops:
  0.6 39.9 %shard_map.77 = (f32[16,760]{1,0:T(8,128)S(1)}, f32[16,760]{1,0:T(8,128)S(1)}) custom-call(bf16[16,9025]{1,0:T(8,128)(2,1)} %bitcast.9, bf16[16,9025]{1,0:T(8,128)(2,1)} %bitcast.10, bf16[16,9025]{1,0:T(8,128)(2,1)} %bitcast.11, f32[16,760]{1,0:T(8,128)} %bitcast.12, s32[1,2]{1,0:T(1,128)} %face_ref.1, f32[16,190]{1,0:T(8,128)} %bitcast.13), custom_call_target="tpu_custom_call" | custom-call | tf_op jit(solution)/shard_map/pallas_call | solution.py:652
  40.5 0.6 %copy.10 = f32[1,16,760]{2,1,0:T(8,128)} copy(f32[1,16,760]{2,1,0:T(8,128)S(1)} %bitcast.8) | data formatting | bytes 97280
  41.1 0.6 %copy.11 = f32[1,16,760]{2,1,0:T(8,128)} copy(f32[1,16,760]{2,1,0:T(8,128)S(1)} %bitcast.7) | data formatting | bytes 97280

commit v6 on v5

--- a/solution.py
+++ b/solution.py
@@ -157,6 +157,8 @@
     kw,
     jw,
     jp,
+    ku,
+    kx,
     hw,
     hsum,
     rho,
@@ -227,7 +229,7 @@
     lax.fori_loop(0, 2 * cells - 1, clear_nodes, 0)
 
     def clear(i, _):
-        for ref in (qw, ew, kw, jw, jp):
+        for ref in (qw, ew, kw, jw, jp, ku, kx):
             ref[i, pl.ds(ROWS, LANES - ROWS), :] = tail
         return 0
 
@@ -423,9 +425,9 @@
     from_before = jnp.maximum(me - 1, 0)
     from_after = jnp.maximum(n - 2 - me, 0)
 
-    def with_pivot(i):
+    def times_pivot(table, i):
         exact = pivot[i]
-        put(jp, i, dot(left_of((jw, i)), jnp.concatenate([exact, exact], axis=0)))
+        return dot(left_of((table, i)), jnp.concatenate([exact, exact], axis=0))
 
     def extended(slot):
         high, low = parts(unpacked(came[slot]))
@@ -446,7 +448,7 @@
         e = multiply(left_of((tb, step)), right_of((ew, step - 1)))
         j = multiply(left_of((jw, back + 1)), right_of((tb, back + 1)))
         h = multiply(left_of((kw, step - 1)), right_of((ew, step - 1)))
-        with_pivot(back + 1)
+        put(jp, back + 1, times_pivot(jw, back + 1))
         put(phi, towards, chained)
         put(kw, step, k)
         put(ew, step, e)
@@ -455,7 +457,7 @@
         return 0
 
     lax.fori_loop(1, cells, tables, 0)
-    with_pivot(0)
+    put(jp, 0, times_pivot(jw, 0))
     put(hw, 0, hsum[...] + multiply(left_of((kw, cells - 1)), right_of((ew, cells - 1))))
 
     between = [(phi, k) for k in range(n)]
@@ -503,18 +505,17 @@
         put(rho, 1, multiply(left_of((rho, 0)), right_of((tb, whole))))
         put(rho, 2, multiply(left_of((tn, whole)), right_of((rho, 0))))
 
-    def inside(turn, left):
-        z = [zs[i] + folded(dot(left, kw[i])) for i in range(cells)]
+    def inside(turn, z):
         source, sums = climb(z[::-1], backward_node, False)
         for p, u in enumerate(descend(source, sums, backward_node)):
             i = cells - 1 - p
             product = dot(stacked_vector(u), pivot[i])
             xs[turn, i] = product[:NR] + product[NR:]
 
-    def complete(turn, entering):
+    def complete(turn, entering, table):
         left = stacked_vector(entering)
         for i in range(cells):
-            xs[turn, i] = xs[turn, i] + folded(dot(left, jp[i]))
+            xs[turn, i] = xs[turn, i] + folded(dot(left, table[i]))
 
     def backward_alone():
         return deep([zs[i] for i in range(cells)], [(ew, i) for i in range(cells)])
@@ -524,8 +525,7 @@
     left = stacked_vector(deep([fcame[0, k] for k in range(n)], between))
     gsend[0] = alone + folded(dot(left, hw[0]))
     send_g(0)
-    send_answers()
-    inside(0, left)
+    inside(0, [z + folded(dot(left, kw[i])) for i, z in enumerate(zs[i] for i in range(cells))])
 
     def chain_back(step, _):
         slot = n - step
@@ -534,8 +534,9 @@
         return 0
 
     lax.fori_loop(1, from_after + 1, chain_back, 0)
+    send_answers()
     wait_g(0)
-    complete(0, deep([gcame[0, k] for k in range(n)], between))
+    complete(0, deep([gcame[0, k] for k in range(n)], between), jp)
 
     def halo_copy(side, other):
         return pltpu.make_async_remote_copy(
@@ -583,7 +584,6 @@
         return 0
 
     lax.fori_loop(1, n, drain, 0)
-    take_answers()
 
     def last_n(m):
         return (tn, node(m, cells, cells - m)) if low_bit(m) == m else (qw, m)
@@ -593,6 +593,20 @@
         if size != m:
             first = node(size, cells, cells - m)
             put(qw, m, multiply(left_of((tn, first)), right_of(last_n(m - size))))
+
+    ku[cells - 1] = kw[cells - 1]
+
+    def respond(step, _):
+        back = cells - 1 - step
+        own = left_of((kw, back))
+        own = own[:, :LANES].astype(F32) + own[:, LANES:].astype(F32)
+        put(ku, back, own + multiply(left_of((ku, back + 1)), right_of((tb, back + 1))))
+        put(kx, back + 1, times_pivot(ku, back + 1))
+        return 0
+
+    lax.fori_loop(1, cells, respond, 0)
+    put(kx, 0, times_pivot(ku, 0))
+    take_answers()
 
     halo_copy(0, high_line).wait_recv()
     halo_copy(1, low_line).wait_recv()
@@ -611,10 +625,11 @@
     keep_alone(*climb([src[i] for i in range(cells)], forward_node, False))
     gsend[1] = backward_alone() + by(leaving, (rho, 1))
     send_g(1)
+    inside(1, [zs[i] for i in range(cells)])
     wait_f(1)
-    left = stacked_vector(deep([fcame[1, k] for k in range(n)], between))
-    inside(1, left)
-    back = by(leaving, (rho, 0)) + folded(dot(left, rho[2]))
+    entering = deep([fcame[1, k] for k in range(n)], between)
+    complete(1, entering, kx)
+    back = by(leaving, (rho, 0)) + by(entering, (rho, 2))
     halo_copy(0, high_line).wait_send()
     halo_copy(1, low_line).wait_send()
 
@@ -632,7 +647,7 @@
 
     lax.fori_loop(1, n, drain_last, 0)
     wait_g(1)
-    complete(1, back + deep([gcame[1, k] for k in range(n)], between))
+    complete(1, back + deep([gcame[1, k] for k in range(n)], between), jp)
     store_cells(xs[1].reshape(cells * NR, LANES), second_ref)
 
 
@@ -663,6 +678,8 @@
             pltpu.VMEM((cells, LANES, LANES), BF16),
             tree,
             tree,
+            weight,
+            weight,
             weight,
             weight,
             weight,

time: 42.2 us -> 44.8 us (1.062)
  Pallas kernels: 39.9 us -> 42.6 us
    pallas_call x1, Pallas kernels: 39.9 us -> 42.6 us  [body(): pl.pallas_call(functools.partial(kernel, n, lines), out_shape=[pltpu.VMEM...]
where the time goes in v6:
time: 44.8 us; the launch traced here: 44.5 us
  Pallas kernels  42.6 us (95%)
  local copies, waits for them, and re-layouts  1.24 us (3%)
  between operations  0.64 us (1%)
    pallas_call x1, Pallas kernels, body(): pl.pallas_call(functools.partial(kernel, n, lines), out_shape=[pltpu.VMEM...  42.6 us
    unnamed x2, local copies, waits for them, and re-layouts  1.24 us

profile of v6, /device:TPU:24, one launch (start us, length us, event | category | flops | bytes accessed | tf_op | source)
XLA Modules:
  0.0 44.5 jit_solution(14702239625214715981)
XLA Ops:
  0.6 42.6 %shard_map.77 = (f32[16,760]{1,0:T(8,128)S(1)}, f32[16,760]{1,0:T(8,128)S(1)}) custom-call(bf16[16,9025]{1,0:T(8,128)(2,1)} %bitcast.9, bf16[16,9025]{1,0:T(8,128)(2,1)} %bitcast.10, bf16[16,9025]{1,0:T(8,128)(2,1)} %bitcast.11, f32[16,760]{1,0:T(8,128)} %bitcast.12, s32[1,2]{1,0:T(1,128)} %face_ref.1, f32[16,190]{1,0:T(8,128)} %bitcast.13), custom_call_target="tpu_custom_call" | custom-call | tf_op jit(solution)/shard_map/pallas_call | solution.py:667
  43.2 0.6 %copy.10 = f32[1,16,760]{2,1,0:T(8,128)} copy(f32[1,16,760]{2,1,0:T(8,128)S(1)} %bitcast.8) | data formatting | bytes 97280
  43.8 0.6 %copy.11 = f32[1,16,760]{2,1,0:T(8,128)} copy(f32[1,16,760]{2,1,0:T(8,128)S(1)} %bitcast.7) | data formatting | bytes 97280

commit v7 on v6

--- a/solution.py
+++ b/solution.py
@@ -525,6 +525,7 @@
     left = stacked_vector(deep([fcame[0, k] for k in range(n)], between))
     gsend[0] = alone + folded(dot(left, hw[0]))
     send_g(0)
+    send_answers()
     inside(0, [z + folded(dot(left, kw[i])) for i, z in enumerate(zs[i] for i in range(cells))])
 
     def chain_back(step, _):
@@ -534,7 +535,6 @@
         return 0
 
     lax.fori_loop(1, from_after + 1, chain_back, 0)
-    send_answers()
     wait_g(0)
     complete(0, deep([gcame[0, k] for k in range(n)], between), jp)
 

time: 44.8 us -> 45 us (level)
  no operation moved by 1% of the time
where the time goes in v7:
time: 45 us; the launch traced here: 44.6 us
  Pallas kernels  42.7 us (95%)
  local copies, waits for them, and re-layouts  1.24 us (3%)
  between operations  0.64 us (1%)
    pallas_call x1, Pallas kernels, body(): pl.pallas_call(functools.partial(kernel, n, lines), out_shape=[pltpu.VMEM...  42.7 us
    unnamed x2, local copies, waits for them, and re-layouts  1.24 us

profile of v7, /device:TPU:24, one launch (start us, length us, event | category | flops | bytes accessed | tf_op | source)
XLA Modules:
  0.0 44.6 jit_solution(8596632691248210590)
XLA Ops:
  0.6 42.7 %shard_map.77 = (f32[16,760]{1,0:T(8,128)S(1)}, f32[16,760]{1,0:T(8,128)S(1)}) custom-call(bf16[16,9025]{1,0:T(8,128)(2,1)} %bitcast.9, bf16[16,9025]{1,0:T(8,128)(2,1)} %bitcast.10, bf16[16,9025]{1,0:T(8,128)(2,1)} %bitcast.11, f32[16,760]{1,0:T(8,128)} %bitcast.12, s32[1,2]{1,0:T(1,128)} %face_ref.1, f32[16,190]{1,0:T(8,128)} %bitcast.13), custom_call_target="tpu_custom_call" | custom-call | tf_op jit(solution)/shard_map/pallas_call | solution.py:667
  43.4 0.6 %copy.10 = f32[1,16,760]{2,1,0:T(8,128)} copy(f32[1,16,760]{2,1,0:T(8,128)S(1)} %bitcast.8) | data formatting | bytes 97280
  44.0 0.6 %copy.11 = f32[1,16,760]{2,1,0:T(8,128)} copy(f32[1,16,760]{2,1,0:T(8,128)S(1)} %bitcast.7) | data formatting | bytes 97280

commit v8 on v5

--- a/solution.py
+++ b/solution.py
@@ -550,8 +550,6 @@
     halo_copy(0, high_line).start()
     halo_copy(1, low_line).start()
 
-    store_cells(xs[0].reshape(cells * NR, LANES), first_ref)
-
     loads[4].wait()
     weights = []
     for place in range(3):
@@ -563,28 +561,6 @@
             )
         weights.append(jnp.concatenate([total, jnp.zeros((cells, LANES - NV), F32)], axis=1))
 
-    def drain(step, _):
-        @pl.when(me + step < n)
-        def _():
-            f_copy(0, step, me + step).wait_send()
-
-        @pl.when(me - step >= 0)
-        def _():
-            g_copy(0, n - step, me - step).wait_send()
-
-        @pl.when((me >= 1) & (me + step < n))
-        def _():
-            map_copy(0, step, me + step).wait_send()
-
-        @pl.when((me <= n - 2) & (me - step >= 0))
-        def _():
-            map_copy(1, n - step, me - step).wait_send()
-
-        return 0
-
-    lax.fori_loop(1, n, drain, 0)
-    take_answers()
-
     def last_n(m):
         return (tn, node(m, cells, cells - m)) if low_bit(m) == m else (qw, m)
 
@@ -593,6 +569,10 @@
         if size != m:
             first = node(size, cells, cells - m)
             put(qw, m, multiply(left_of((tn, first)), right_of(last_n(m - size))))
+
+    @pl.when(me >= n // 2)
+    def _():
+        take_answers()
 
     halo_copy(0, high_line).wait_recv()
     halo_copy(1, low_line).wait_recv()
@@ -608,9 +588,15 @@
     leaving = deep([src[i] for i in range(cells)], [last_n(cells - i) for i in range(cells)])
     fsend[1] = leaving
     send_f(1)
+
+    @pl.when(me < n // 2)
+    def _():
+        take_answers()
+
     keep_alone(*climb([src[i] for i in range(cells)], forward_node, False))
     gsend[1] = backward_alone() + by(leaving, (rho, 1))
     send_g(1)
+    store_cells(xs[0].reshape(cells * NR, LANES), first_ref)
     wait_f(1)
     left = stacked_vector(deep([fcame[1, k] for k in range(n)], between))
     inside(1, left)
@@ -618,19 +604,29 @@
     halo_copy(0, high_line).wait_send()
     halo_copy(1, low_line).wait_send()
 
-    def drain_last(step, _):
+    def drain(step, _):
         @pl.when(me + step < n)
         def _():
+            f_copy(0, step, me + step).wait_send()
             f_copy(1, step, me + step).wait_send()
+
+        @pl.when((me >= 1) & (me + step < n))
+        def _():
+            map_copy(0, step, me + step).wait_send()
+
+        @pl.when((me <= n - 2) & (me - step >= 0))
+        def _():
+            map_copy(1, n - step, me - step).wait_send()
 
         @pl.when(me - step >= 0)
         def _():
+            g_copy(0, n - step, me - step).wait_send()
             g_copy(1, n - step, me - step).wait_send()
             answer_copy(n - step, me - step).wait_send()
 
         return 0
 
-    lax.fori_loop(1, n, drain_last, 0)
+    lax.fori_loop(1, n, drain, 0)
     wait_g(1)
     complete(1, back + deep([gcame[1, k] for k in range(n)], between))
     store_cells(xs[1].reshape(cells * NR, LANES), second_ref)

time: 42.2 us -> 42.3 us (level)
  no operation moved by 1% of the time
where the time goes in v8:
time: 42.3 us; the launch traced here: 41.8 us
  Pallas kernels  39.9 us (94%)
  local copies, waits for them, and re-layouts  1.24 us (3%)
  between operations  0.64 us (2%)
    pallas_call x1, Pallas kernels, body(): pl.pallas_call(functools.partial(kernel, n, lines), out_shape=[pltpu.VMEM...  39.9 us
    unnamed x2, local copies, waits for them, and re-layouts  1.24 us

profile of v8, /device:TPU:24, one launch (start us, length us, event | category | flops | bytes accessed | tf_op | source)
XLA Modules:
  0.0 41.8 jit_solution(15814131745879855814)
XLA Ops:
  0.6 39.9 %shard_map.77 = (f32[16,760]{1,0:T(8,128)S(1)}, f32[16,760]{1,0:T(8,128)S(1)}) custom-call(bf16[16,9025]{1,0:T(8,128)(2,1)} %bitcast.9, bf16[16,9025]{1,0:T(8,128)(2,1)} %bitcast.10, bf16[16,9025]{1,0:T(8,128)(2,1)} %bitcast.11, f32[16,760]{1,0:T(8,128)} %bitcast.12, s32[1,2]{1,0:T(1,128)} %face_ref.1, f32[16,190]{1,0:T(8,128)} %bitcast.13), custom_call_target="tpu_custom_call" | custom-call | tf_op jit(solution)/shard_map/pallas_call | solution.py:648
  40.6 0.6 %copy.10 = f32[1,16,760]{2,1,0:T(8,128)} copy(f32[1,16,760]{2,1,0:T(8,128)S(1)} %bitcast.8) | data formatting | bytes 97280
  41.2 0.6 %copy.11 = f32[1,16,760]{2,1,0:T(8,128)} copy(f32[1,16,760]{2,1,0:T(8,128)S(1)} %bitcast.7) | data formatting | bytes 97280

commit v9 on v8

--- a/solution.py
+++ b/solution.py
@@ -570,9 +570,7 @@
             first = node(size, cells, cells - m)
             put(qw, m, multiply(left_of((tn, first)), right_of(last_n(m - size))))
 
-    @pl.when(me >= n // 2)
-    def _():
-        take_answers()
+    take_answers()
 
     halo_copy(0, high_line).wait_recv()
     halo_copy(1, low_line).wait_recv()
@@ -588,10 +586,6 @@
     leaving = deep([src[i] for i in range(cells)], [last_n(cells - i) for i in range(cells)])
     fsend[1] = leaving
     send_f(1)
-
-    @pl.when(me < n // 2)
-    def _():
-        take_answers()
 
     keep_alone(*climb([src[i] for i in range(cells)], forward_node, False))
     gsend[1] = backward_alone() + by(leaving, (rho, 1))

time: 42.3 us -> 42.4 us (level)
  no operation moved by 1% of the time
where the time goes in v9:
time: 42.4 us; the launch traced here: 41.9 us
  Pallas kernels  40.1 us (95%)
  local copies, waits for them, and re-layouts  1.24 us (3%)
  between operations  0.64 us (2%)
    pallas_call x1, Pallas kernels, body(): pl.pallas_call(functools.partial(kernel, n, lines), out_shape=[pltpu.VMEM...  40.1 us
    unnamed x2, local copies, waits for them, and re-layouts  1.24 us

profile of v9, /device:TPU:24, one launch (start us, length us, event | category | flops | bytes accessed | tf_op | source)
XLA Modules:
  0.0 41.9 jit_solution(16226445777210315491)
XLA Ops:
  0.6 40.1 %shard_map.77 = (f32[16,760]{1,0:T(8,128)S(1)}, f32[16,760]{1,0:T(8,128)S(1)}) custom-call(bf16[16,9025]{1,0:T(8,128)(2,1)} %bitcast.9, bf16[16,9025]{1,0:T(8,128)(2,1)} %bitcast.10, bf16[16,9025]{1,0:T(8,128)(2,1)} %bitcast.11, f32[16,760]{1,0:T(8,128)} %bitcast.12, s32[1,2]{1,0:T(1,128)} %face_ref.1, f32[16,190]{1,0:T(8,128)} %bitcast.13), custom_call_target="tpu_custom_call" | custom-call | tf_op jit(solution)/shard_map/pallas_call | solution.py:642
  40.7 0.6 %copy.10 = f32[1,16,760]{2,1,0:T(8,128)} copy(f32[1,16,760]{2,1,0:T(8,128)S(1)} %bitcast.8) | data formatting | bytes 97280
  41.3 0.6 %copy.11 = f32[1,16,760]{2,1,0:T(8,128)} copy(f32[1,16,760]{2,1,0:T(8,128)S(1)} %bitcast.7) | data formatting | bytes 97280
